TPU v7x, 32 devices: a whole 2x2x4 slice. The times are simulated.
32 devices in a mesh: gx: 8 (over z, x), gy: 4 (over y, core).
Axes of the slice: x: 2, y: 2, z: 4, core: 2. Of those that a mesh axis runs over, the one named last changes fastest.
Arguments:
- source: float32 [6, 64, 64, 128], P(None, 'gx', 'gy'), may hold values from -6 to 6
- cell_class: int32 [64, 64, 128], P('gx', 'gy'), may hold values from 0 to 7
- class_conductivity: float32 [8], replicated, may hold values from 0.1 to 3
- layer_of_depth: int32 [64], replicated, may hold values from 0 to 7
- inverses: float32 [8, 192, 192], replicated, as said below
Outputs:
- correction: float32 [6, 64, 64, 128], P(None, 'gx', 'gy')
Inputs may be any that keep to these rules, and one draw needn't show every extreme that they name: `inverses`: each matrix has a positive diagonal.
All inputs are finite; a program needn't handle non-finite values.
Results may differ from a plain program's by a relative error of at most 0.000054.
Values sent between devices are 32-bit elements; how exact they have to be, the bound alone decides.
A program may use at most 128 MiB of HBM per device.

v0:
```python
import functools

import jax
import jax.numpy as jnp
from jax import lax
from jax.experimental import pallas as pl
from jax.experimental.pallas import tpu as pltpu
from jax.sharding import PartitionSpec as P

damping = 0.8
MESH = pl.DeviceIdType.MESH
f32 = jnp.float32
bf16 = jnp.bfloat16


def roll(x, shift, axis):
    shift = shift % x.shape[axis]
    return x if shift == 0 else pltpu.roll(x, shift, axis)


def iota(shape, axis):
    return lax.broadcasted_iota(jnp.int32, shape, axis)


def split(x):
    hi = x.astype(bf16)
    return hi, (x - hi.astype(f32)).astype(bf16)


def dot(a, b):
    return jnp.dot(a, b, preferred_element_type=f32)


def permute(x, matrix):
    hi, lo = split(x)
    return dot(hi, matrix) + dot(lo, matrix)


def pick_rows(x, places):
    row = iota(x.shape, 1)
    out = jnp.zeros_like(x)
    for shift in range(8):
        rows = [s for s in range(8) if places[s] is not None and (s - places[s]) % 8 == shift]
        if rows:
            mask = functools.reduce(jnp.logical_or, [row == s for s in rows])
            out = jnp.where(mask, roll(x, shift, 1), out)
    return out


def pair_rows(x):
    tiles = []
    for t in range(x.shape[1] // 16):
        low, high = x[:, 16 * t : 16 * t + 8], x[:, 16 * t + 8 : 16 * t + 16]
        low = low + roll(low, 7, 1)
        high = high + roll(high, 7, 1)
        tiles.append(pick_rows(low, [0, 2, 4, 6] + [None] * 4) + pick_rows(high, [None] * 4 + [0, 2, 4, 6]))
    return jnp.concatenate(tiles, axis=1)


def repeat_rows(x):
    tiles = []
    for t in range(x.shape[1] // 8):
        tile = x[:, 8 * t : 8 * t + 8]
        tiles.append(pick_rows(tile, [0, 0, 1, 1, 2, 2, 3, 3]))
        tiles.append(pick_rows(tile, [4, 4, 5, 5, 6, 6, 7, 7]))
    return jnp.concatenate(tiles, axis=1)


def first_half(shape, half):
    lane = iota(shape, len(shape) - 1)
    mask = lane < half
    for start in range(2 * half, shape[-1], 2 * half):
        mask = mask | ((lane >= start) & (lane < start + half))
    return mask


def swap_tiles(v0, v1):
    low = iota(v0.shape, 1) < 4
    return jnp.where(low, v0, roll(v1, 4, 1)), jnp.where(low, roll(v0, 4, 1), v1)


def swap_lanes(a, b, half):
    mask = first_half(a.shape, half)
    return jnp.where(mask, a, roll(b, half, 1)), jnp.where(mask, roll(a, -half, 1), b)


def smooth(field, out_ref, w_hi, w_lo, ids, half, scale):
    comps, sx, sy, nz = field.shape
    rows = comps * 16
    pairs = [(xb, p) for xb in range(sx // 4) for p in range(sy // 8)]
    columns = []
    for xb, p in pairs:
        v = field[:, 4 * xb : 4 * xb + 4, 8 * p : 8 * p + 8, :].reshape(comps * 2, 2, 8, nz)
        u0, u1 = swap_tiles(v[:, 0], v[:, 1])
        even, odd = swap_lanes(u0.reshape(rows, nz), u1.reshape(rows, nz), half)
        columns.append(jnp.concatenate([even, odd], axis=0))
    x = jnp.concatenate(columns, axis=1)
    hi, lo = split(x)
    size = 2 * rows
    every = dot(w_hi[...], hi) + dot(w_lo[...], hi) + dot(w_hi[...], lo)
    ids = jnp.concatenate([ids] * len(pairs), axis=1)
    total = jnp.zeros_like(x)
    for layer in range(w_hi.shape[0] // size):
        total = jnp.where(ids == layer, every[layer * size : (layer + 1) * size], total)
    total = total * scale
    for at, (xb, p) in enumerate(pairs):
        block = total[:, at * nz : (at + 1) * nz]
        u0, u1 = swap_lanes(block[:rows], block[rows:], half)
        v0, v1 = swap_tiles(u0.reshape(comps * 2, 8, nz), u1.reshape(comps * 2, 8, nz))
        v = jnp.stack([v0, v1], axis=1).reshape(comps, 4, 8, nz)
        out_ref[:, 4 * xb : 4 * xb + 4, 8 * p : 8 * p + 8, :] = v


def beside_z_fine(u):
    nz = u.shape[-1]
    q = nz // 4
    lane = iota(u.shape, u.ndim - 1)
    ax = u.ndim - 1
    other = jnp.where(
        lane < 2 * q,
        jnp.where(lane < q, roll(u, q + 1, ax), roll(u, -q, ax)),
        jnp.where(lane < 3 * q, roll(u, q, ax), roll(u, -q - 1, ax)),
    )
    other = jnp.where((lane == 0) | (lane == nz - 1), 0.0, other)
    return roll(u, 2 * q, ax) + other


def beside_z_coarse(u):
    nz = u.shape[-1]
    q = nz // 4
    lane = iota(u.shape, u.ndim - 1)
    ax = u.ndim - 1
    mask = first_half(u.shape, q)
    total = jnp.where(mask, roll(u, -q, ax), roll(u, q, ax))
    other = jnp.where(mask, roll(u, 1 - q, ax), roll(u, q - 1, ax))
    edge = (lane == 0) | (lane == 2 * q - 1) | (lane == 2 * q) | (lane == nz - 1)
    return total + jnp.where(edge, 0.0, other)


def residual(b, u, sigma, beside_z, factor):
    comps, sx, sy, nz = u.shape
    half = comps // 2
    flat = u.reshape(comps * sx, sy, nz)
    row = iota(flat.shape, 1)
    near = jnp.where(row == 0, 0.0, roll(flat, 1, 1)) + jnp.where(row == sy - 1, 0.0, roll(flat, -1, 1))
    near = (near + beside_z(flat)).reshape(u.shape)
    zero = jnp.zeros((comps, 1, sy, nz), f32)
    near = near + jnp.concatenate([zero, u[:, :-1]], axis=1) + jnp.concatenate([u[:, 1:], zero], axis=1)
    out = b - (6.0 * u - near) * factor
    turned = jnp.concatenate([sigma[None] * u[half:], -(sigma[None] * u[:half])], axis=0)
    return out + turned


def add_faces(r, faces_x, faces_y, factor):
    comps, sx, sy, nz = r.shape
    row = iota((comps * sx, sy, nz), 1)
    flat = r.reshape(comps * sx, sy, nz)
    flat = flat + jnp.where(row == 0, faces_y[0] * factor, 0.0) + jnp.where(row == sy - 1, faces_y[1] * factor, 0.0)
    r = flat.reshape(r.shape)
    low = r[:, :1] + faces_x[0][:, None] * factor
    high = r[:, sx - 1 :] + faces_x[1][:, None] * factor
    return jnp.concatenate([low, r[:, 1 : sx - 1], high], axis=1)


def restrict(u):
    comps, sx, sy, nz = u.shape
    v = u.reshape(comps * sx // 2, 2, sy, nz)
    v = v[:, 0] + v[:, 1]
    v = pair_rows(v)
    v = (v + roll(v, nz // 2, 2)) * 0.125
    return v.reshape(comps, sx // 2, sy // 2, nz)


def kernel(
    axes, sizes, src, cls, cond, depth, inv, out,
    w_hi, w_lo, b0, x0, r0, sig0, sig1, b1, x1, r1, d1,
    send_x, recv_x, send_y, recv_y, csend_x, crecv_x, csend_y, crecv_y, send_sem, recv_sem,
):
    comps, sx, sy, nz = src.shape
    me = [lax.axis_index(a) for a in axes]
    has = [me[0] > 0, me[0] < sizes[0] - 1, me[1] > 0, me[1] < sizes[1] - 1]

    def device(d):
        n = sizes[d // 2]
        return {axes[d // 2]: lax.rem(me[d // 2] + (n - 1 if d % 2 == 0 else 1), n)}

    barrier = pltpu.get_barrier_semaphore()
    for d in range(4):
        @pl.when(has[d])
        def _(d=d):
            pl.semaphore_signal(barrier, inc=1, device_id=device(d), device_id_type=MESH)

        @pl.when(jnp.logical_not(has[d]))
        def _(d=d):
            for ref in [(recv_x, crecv_x), (recv_y, crecv_y)][d // 2]:
                if ref is recv_x or ref is recv_y:
                    ref[d % 2] = jnp.zeros(ref.shape[1:], f32)
                else:
                    for e in range(2):
                        ref[e, d % 2] = jnp.zeros(ref.shape[2:], f32)

    def copy(e, d):
        if d < 2:
            s, r = (send_x, recv_x) if e == 0 else (csend_x.at[e - 1], crecv_x.at[e - 1])
        else:
            s, r = (send_y, recv_y) if e == 0 else (csend_y.at[e - 1], crecv_y.at[e - 1])
        k = d % 2
        return pltpu.make_async_remote_copy(
            src_ref=s.at[k], dst_ref=r.at[1 - k], send_sem=send_sem.at[e, d], recv_sem=recv_sem.at[e, d ^ 1],
            device_id=device(d), device_id_type=MESH,
        )

    def start(e, u):
        c, ux, uy, _ = u.shape
        sxr, syr = (send_x, send_y) if e == 0 else (csend_x.at[e - 1], csend_y.at[e - 1])
        sxr[0] = u[:, 0]
        sxr[1] = u[:, ux - 1]
        flat = u.reshape(c * ux, uy, nz)
        syr[0] = flat[:, 0:1]
        syr[1] = flat[:, uy - 1 : uy]
        for d in range(4):
            @pl.when(has[d])
            def _(d=d):
                copy(e, d).start()

    def finish(e):
        for d in range(4):
            @pl.when(has[d])
            def _(d=d):
                copy(e, d ^ 1).wait_recv()
                copy(e, d).wait_send()

    q = nz // 4
    def z_of(lane):
        zi = jnp.where(lane >= 2 * q, 1, 0)
        rest = lane - 2 * q * zi
        zic = jnp.where(rest >= q, 1, 0)
        return 4 * (rest - q * zic) + 2 * zic + zi
    to_lanes = jnp.where(iota((nz, nz), 0) == z_of(iota((nz, nz), 1)), 1.0, 0.0).astype(bf16)
    from_lanes = jnp.where(iota((nz, nz), 1) == z_of(iota((nz, nz), 0)), 1.0, 0.0).astype(bf16)

    lane = iota((1, nz), 1)
    zb = z_of(lane - jnp.where(lane >= 2 * q, 2 * q, 0)) // 2
    ids0 = jnp.zeros((1, nz), jnp.int32)
    for k in range(depth.shape[0]):
        ids0 = jnp.where(zb == k, depth[k], ids0)
    ids1 = jnp.where(first_half((1, nz), q), ids0, roll(ids0, q, 1))

    layers, size, _ = inv.shape
    mid = size // 2
    def k_of(j):
        return jnp.where(j < mid, 2 * j, 2 * (j - mid) + 1)
    right = jnp.where(iota((size, size), 0) == k_of(iota((size, size), 1)), 1.0, 0.0).astype(bf16)
    left = jnp.where(iota((size, size), 1) == k_of(iota((size, size), 0)), 1.0, 0.0).astype(bf16)
    for part, ref in zip(split(inv[...].reshape(layers * size, size)), (w_hi, w_lo)):
        turned = dot(part, right).astype(bf16)
        for layer in range(layers):
            at = slice(layer * size, (layer + 1) * size)
            ref[at, :] = dot(left, turned[at]).astype(bf16)

    b0[...] = permute(src[...].reshape(-1, nz), to_lanes).reshape(src.shape)
    kinds = dot(cls[...].reshape(-1, nz).astype(f32).astype(bf16), to_lanes)
    sigma = jnp.zeros_like(kinds)
    for k in range(cond.shape[0]):
        sigma = jnp.where(kinds == float(k), cond[k], sigma)
    sigma = sigma.reshape(sx, sy, nz)
    sig0[...] = sigma
    sig1[...] = restrict(sigma[None])[0]

    smooth(b0[...], x0, w_hi, w_lo, ids0, nz // 2, damping)
    pl.semaphore_wait(barrier, sum(jnp.where(h, 1, 0) for h in has))
    start(0, x0[...])
    r0[...] = residual(b0[...], x0[...], sig0[...], beside_z_fine, 1.0)
    finish(0)
    b1[...] = restrict(add_faces(r0[...], recv_x, recv_y, 1.0))

    smooth(b1[...], x1, w_hi, w_lo, ids1, q, damping * 4.0)
    start(1, x1[...])
    r1[...] = residual(b1[...], x1[...], sig1[...], beside_z_coarse, 0.25)
    finish(1)
    smooth(add_faces(r1[...], crecv_x.at[0], crecv_y.at[0], 0.25), d1, w_hi, w_lo, ids1, q, damping * 4.0)
    xc = x1[...] + d1[...]
    start(2, xc)
    cx, cy = sx // 2, sy // 2
    spread = repeat_rows(xc.reshape(comps * cx, cy, nz)).reshape(comps, cx, 1, sy, nz)
    spread = jnp.concatenate([spread, spread], axis=2).reshape(src.shape)
    x0[...] = x0[...] + spread
    r0[...] = residual(b0[...], x0[...], sig0[...], beside_z_fine, 1.0)
    finish(2)
    faces_x = [recv_x[k] + repeat_rows(crecv_x[1, k]) for k in range(2)]
    faces_y = []
    for k in range(2):
        face = crecv_y[1, k].reshape(comps * cx, 1, 1, nz)
        face = jnp.concatenate([face, face], axis=1).reshape(comps * sx, 1, nz)
        faces_y.append(recv_y[k] + face)
    smooth(add_faces(r0[...], faces_x, faces_y, 1.0), r0, w_hi, w_lo, ids0, nz // 2, damping)
    out[...] = permute((x0[...] + r0[...]).reshape(-1, nz), from_lanes).reshape(out.shape)


def solution(mesh):
    axes = ("gx", "gy")
    sizes = tuple(mesh.shape[a] for a in axes)

    def per_device(source, cell_class, class_conductivity, layer_of_depth, inverses):
        comps, sx, sy, nz = source.shape
        layers, size, _ = inverses.shape
        cx, cy = sx // 2, sy // 2
        vmem = pl.BlockSpec(memory_space=pltpu.VMEM)
        smem = pl.BlockSpec(memory_space=pltpu.SMEM)
        fine, coarse = (comps, sx, sy, nz), (comps, cx, cy, nz)
        scratch = [
            ((layers * size, size), bf16), ((layers * size, size), bf16),
            (fine, f32), (fine, f32), (fine, f32), ((sx, sy, nz), f32), ((cx, cy, nz), f32),
            (coarse, f32), (coarse, f32), (coarse, f32), (coarse, f32),
        ]
        scratch += [((2, comps, sy, nz), f32)] * 2 + [((2, comps * sx, 1, nz), f32)] * 2
        scratch += [((2, 2, comps, cy, nz), f32)] * 2 + [((2, 2, comps * cx, 1, nz), f32)] * 2
        return pl.pallas_call(
            functools.partial(kernel, axes, sizes),
            out_shape=jax.ShapeDtypeStruct(source.shape, f32),
            in_specs=[vmem, vmem, smem, smem, vmem],
            out_specs=vmem,
            scratch_shapes=[pltpu.VMEM(s, t) for s, t in scratch]
            + [pltpu.SemaphoreType.DMA((3, 4)), pltpu.SemaphoreType.DMA((3, 4))],
            compiler_params=pltpu.CompilerParams(
                collective_id=0, has_side_effects=True, vmem_limit_bytes=50 * 2**20
            ),
        )(source, cell_class, class_conductivity, layer_of_depth, inverses)

    return jax.shard_map(
        per_device,
        mesh=mesh,
        in_specs=(P(None, "gx", "gy", None), P("gx", "gy", None), P(), P(), P()),
        out_specs=P(None, "gx", "gy", None),
        check_vma=False,
    )
```

profile of v0, /device:TPU:0, one launch (start us, length us, event | category | flops | bytes accessed | tf_op | source)
XLA Modules:
  0.0 26.4 jit_solution(1339404902478184859)
XLA Ops:
  0.0 0.0 copy-start
  0.0 1.4 %copy-done = f32[8,192,192]{2,1,0:T(8,128)S(1)} copy-done((f32[8,192,192]{2,1,0:T(8,128)S(1)}, f32[8,192,192]{2,1,0:T(8,128)}, u32[]{:S(2)}) %copy-start) | copy-done | bytes 1179672
  1.4 0.0 copy-start.1
  1.4 1.0 %copy-done.1 = f32[6,8,16,128]{3,2,1,0:T(8,128)S(1)} copy-done((f32[6,8,16,128]{3,2,1,0:T(8,128)S(1)}, f32[6,8,16,128]{3,2,1,0:T(8,128)}, u32[]{:S(2)}) %copy-start.1) | copy-done | bytes 393240
  2.4 0.0 copy-start.2
  2.4 0.8 %copy-done.2 = s32[8,16,128]{2,1,0:T(8,128)S(1)} copy-done((s32[8,16,128]{2,1,0:T(8,128)S(1)}, s32[8,16,128]{2,1,0:T(8,128)}, u32[]{:S(2)}) %copy-start.2) | copy-done | bytes 65560
  3.2 0.0 copy-start.3
  3.2 0.7 %copy-done.3 = f32[8]{0:T(128)S(1)} copy-done((f32[8]{0:T(128)S(1)}, f32[8]{0:T(128)}, u32[]{:S(2)}) %copy-start.3) | copy-done | bytes 56
  3.9 0.0 copy-start.4
  3.9 0.7 %copy-done.4 = s32[64]{0:T(128)S(1)} copy-done((s32[64]{0:T(128)S(1)}, s32[64]{0:T(128)}, u32[]{:S(2)}) %copy-start.4) | copy-done | bytes 280
  4.6 21.1 %shard_map.55 = f32[6,8,16,128]{3,2,1,0:T(8,128)S(1)} custom-call(f32[6,8,16,128]{3,2,1,0:T(8,128)S(1)} %copy-done.1, s32[8,16,128]{2,1,0:T(8,128)S(1)} %copy-done.2, f32[8]{0:T(128)S(1)} %copy-done.3, s32[64]{0:T(128)S(1)} %copy-done.4, f32[8,192,192]{2,1,0:T(8,128)S(1)} %copy-done), custom_call_target="tpu_custom_call" | custom-call | tf_op jit(solution)/shard_map/pallas_call | solution.py:318
  25.7 0.7 %copy.7 = f32[6,8,16,128]{3,2,1,0:T(8,128)} copy(f32[6,8,16,128]{3,2,1,0:T(8,128)S(1)} %shard_map.55) | data formatting | bytes 786432
Async XLA Ops:
  0.0 1.4 %copy-start = (f32[8,192,192]{2,1,0:T(8,128)S(1)}, f32[8,192,192]{2,1,0:T(8,128)}, u32[]{:S(2)}) copy-start(f32[8,192,192]{2,1,0:T(8,128)} %inv.1) | copy-start | bytes 3538948
  1.4 1.0 %copy-start.1 = (f32[6,8,16,128]{3,2,1,0:T(8,128)S(1)}, f32[6,8,16,128]{3,2,1,0:T(8,128)}, u32[]{:S(2)}) copy-start(f32[6,8,16,128]{3,2,1,0:T(8,128)} %src.1) | copy-start | bytes 1179652
  2.4 0.8 %copy-start.2 = (s32[8,16,128]{2,1,0:T(8,128)S(1)}, s32[8,16,128]{2,1,0:T(8,128)}, u32[]{:S(2)}) copy-start(s32[8,16,128]{2,1,0:T(8,128)} %cls.1) | copy-start | bytes 196612
  3.2 0.7 %copy-start.3 = (f32[8]{0:T(128)S(1)}, f32[8]{0:T(128)}, u32[]{:S(2)}) copy-start(f32[8]{0:T(128)} %cond.1) | copy-start | bytes 100
  3.9 0.7 %copy-start.4 = (s32[64]{0:T(128)S(1)}, s32[64]{0:T(128)}, u32[]{:S(2)}) copy-start(s32[64]{0:T(128)} %depth.1) | copy-start | bytes 772
where the time goes:
time: 26.7 us; the launch traced here: 26.4 us
  Pallas kernels  21.1 us (79%)
  local copies, waits for them, and re-layouts  5.3 us (20%)
    pallas_call x1, Pallas kernels, per_device(): pl.pallas_call(functools.partial(kernel, axes, sizes), out_shape=jax.Shap...  21.1 us
    unnamed x11, local copies, waits for them, and re-layouts  5.3 us

commit v1 on v0

--- a/solution.py
+++ b/solution.py
@@ -84,28 +84,44 @@
     return jnp.where(mask, a, roll(b, half, 1)), jnp.where(mask, roll(a, -half, 1), b)
 
 
-def smooth(field, out_ref, w_hi, w_lo, ids, half, scale):
+def masked(x, ids, layers):
+    tiles = x.reshape(-1, 16, x.shape[1])
+    out = []
+    for layer in range(layers):
+        mask = jnp.broadcast_to(jnp.where(ids == layer, 1.0, 0.0), (16, x.shape[1])).astype(bf16)
+        out.append((tiles * mask[None]).reshape(x.shape))
+    return jnp.concatenate(out, axis=0)
+
+
+def smooth(field, out_ref, w, ids, half, scale, block_in, block_out):
     comps, sx, sy, nz = field.shape
     rows = comps * 16
+    size = 2 * rows
+    layers = w.shape[1] // size
     pairs = [(xb, p) for xb in range(sx // 4) for p in range(sy // 8)]
-    columns = []
-    for xb, p in pairs:
+    for at, (xb, p) in enumerate(pairs):
         v = field[:, 4 * xb : 4 * xb + 4, 8 * p : 8 * p + 8, :].reshape(comps * 2, 2, 8, nz)
         u0, u1 = swap_tiles(v[:, 0], v[:, 1])
         even, odd = swap_lanes(u0.reshape(rows, nz), u1.reshape(rows, nz), half)
-        columns.append(jnp.concatenate([even, odd], axis=0))
-    x = jnp.concatenate(columns, axis=1)
-    hi, lo = split(x)
-    size = 2 * rows
-    every = dot(w_hi[...], hi) + dot(w_lo[...], hi) + dot(w_hi[...], lo)
+        block_in[at, pl.ds(0, rows, stride=2), :] = even
+        block_in[at, pl.ds(1, rows, stride=2), :] = odd
+    n = len(pairs) * nz
+    hi, lo = split(jnp.concatenate([block_in[at] for at in range(len(pairs))], axis=1))
     ids = jnp.concatenate([ids] * len(pairs), axis=1)
-    total = jnp.zeros_like(x)
-    for layer in range(w_hi.shape[0] // size):
-        total = jnp.where(ids == layer, every[layer * size : (layer + 1) * size], total)
+    if n < 256:
+        x = masked(jnp.concatenate([hi, lo], axis=1), jnp.concatenate([ids, ids], axis=1), layers)
+        total = dot(w[...], x)
+        total = total[:size] + total[size:]
+        total = total[:, :n] + total[:, n:]
+    else:
+        total = dot(w[...], masked(hi, ids, layers))
+        total = total[:size] + total[size:] + dot(w[:size, :], masked(lo, ids, layers))
     total = total * scale
     for at, (xb, p) in enumerate(pairs):
-        block = total[:, at * nz : (at + 1) * nz]
-        u0, u1 = swap_lanes(block[:rows], block[rows:], half)
+        block_out[at] = total[:, at * nz : (at + 1) * nz]
+        even = block_out[at, pl.ds(0, rows, stride=2), :]
+        odd = block_out[at, pl.ds(1, rows, stride=2), :]
+        u0, u1 = swap_lanes(even, odd, half)
         v0, v1 = swap_tiles(u0.reshape(comps * 2, 8, nz), u1.reshape(comps * 2, 8, nz))
         v = jnp.stack([v0, v1], axis=1).reshape(comps, 4, 8, nz)
         out_ref[:, 4 * xb : 4 * xb + 4, 8 * p : 8 * p + 8, :] = v
@@ -172,11 +188,15 @@
 
 
 def kernel(
-    axes, sizes, src, cls, cond, depth, inv, out,
-    w_hi, w_lo, b0, x0, r0, sig0, sig1, b1, x1, r1, d1,
+    axes, sizes, src_hbm, cls_hbm, cond_hbm, depth_hbm, inv_hbm, out,
+    src, cls, cond, depth, inv, in_sem, block_in, block_out, w, b0, x0, r0, sig0, sig1, b1, x1, r1, d1,
     send_x, recv_x, send_y, recv_y, csend_x, crecv_x, csend_y, crecv_y, send_sem, recv_sem,
 ):
     comps, sx, sy, nz = src.shape
+    named = ((src_hbm, src), (cls_hbm, cls), (cond_hbm, cond), (depth_hbm, depth), (inv_hbm, inv))
+    loads = [pltpu.make_async_copy(a, b, in_sem.at[i]) for i, (a, b) in enumerate(named)]
+    for load in loads:
+        load.start()
     me = [lax.axis_index(a) for a in axes]
     has = [me[0] > 0, me[0] < sizes[0] - 1, me[1] > 0, me[1] < sizes[1] - 1]
 
@@ -239,6 +259,19 @@
     to_lanes = jnp.where(iota((nz, nz), 0) == z_of(iota((nz, nz), 1)), 1.0, 0.0).astype(bf16)
     from_lanes = jnp.where(iota((nz, nz), 1) == z_of(iota((nz, nz), 0)), 1.0, 0.0).astype(bf16)
 
+    loads[0].wait()
+    b0[...] = permute(src[...].reshape(-1, nz), to_lanes).reshape(src.shape)
+    loads[1].wait()
+    kinds = dot(cls[...].reshape(-1, nz).astype(f32).astype(bf16), to_lanes)
+    loads[2].wait()
+    sigma = jnp.zeros_like(kinds)
+    for k in range(cond.shape[0]):
+        sigma = jnp.where(kinds == float(k), cond[k], sigma)
+    sigma = sigma.reshape(sx, sy, nz)
+    sig0[...] = sigma
+    sig1[...] = restrict(sigma[None])[0]
+
+    loads[3].wait()
     lane = iota((1, nz), 1)
     zb = z_of(lane - jnp.where(lane >= 2 * q, 2 * q, 0)) // 2
     ids0 = jnp.zeros((1, nz), jnp.int32)
@@ -246,39 +279,24 @@
         ids0 = jnp.where(zb == k, depth[k], ids0)
     ids1 = jnp.where(first_half((1, nz), q), ids0, roll(ids0, q, 1))
 
+    loads[4].wait()
     layers, size, _ = inv.shape
-    mid = size // 2
-    def k_of(j):
-        return jnp.where(j < mid, 2 * j, 2 * (j - mid) + 1)
-    right = jnp.where(iota((size, size), 0) == k_of(iota((size, size), 1)), 1.0, 0.0).astype(bf16)
-    left = jnp.where(iota((size, size), 1) == k_of(iota((size, size), 0)), 1.0, 0.0).astype(bf16)
-    for part, ref in zip(split(inv[...].reshape(layers * size, size)), (w_hi, w_lo)):
-        turned = dot(part, right).astype(bf16)
-        for layer in range(layers):
-            at = slice(layer * size, (layer + 1) * size)
-            ref[at, :] = dot(left, turned[at]).astype(bf16)
-
-    b0[...] = permute(src[...].reshape(-1, nz), to_lanes).reshape(src.shape)
-    kinds = dot(cls[...].reshape(-1, nz).astype(f32).astype(bf16), to_lanes)
-    sigma = jnp.zeros_like(kinds)
-    for k in range(cond.shape[0]):
-        sigma = jnp.where(kinds == float(k), cond[k], sigma)
-    sigma = sigma.reshape(sx, sy, nz)
-    sig0[...] = sigma
-    sig1[...] = restrict(sigma[None])[0]
-
-    smooth(b0[...], x0, w_hi, w_lo, ids0, nz // 2, damping)
+    hi, lo = split(jnp.concatenate([inv[layer] for layer in range(layers)], axis=1))
+    w[:size, :] = hi
+    w[size:, :] = lo
+
+    smooth(b0[...], x0, w, ids0, nz // 2, damping, block_in, block_out)
     pl.semaphore_wait(barrier, sum(jnp.where(h, 1, 0) for h in has))
     start(0, x0[...])
     r0[...] = residual(b0[...], x0[...], sig0[...], beside_z_fine, 1.0)
     finish(0)
     b1[...] = restrict(add_faces(r0[...], recv_x, recv_y, 1.0))
 
-    smooth(b1[...], x1, w_hi, w_lo, ids1, q, damping * 4.0)
+    smooth(b1[...], x1, w, ids1, q, damping * 4.0, block_in, block_out)
     start(1, x1[...])
     r1[...] = residual(b1[...], x1[...], sig1[...], beside_z_coarse, 0.25)
     finish(1)
-    smooth(add_faces(r1[...], crecv_x.at[0], crecv_y.at[0], 0.25), d1, w_hi, w_lo, ids1, q, damping * 4.0)
+    smooth(add_faces(r1[...], crecv_x.at[0], crecv_y.at[0], 0.25), d1, w, ids1, q, damping * 4.0, block_in, block_out)
     xc = x1[...] + d1[...]
     start(2, xc)
     cx, cy = sx // 2, sy // 2
@@ -293,7 +311,7 @@
         face = crecv_y[1, k].reshape(comps * cx, 1, 1, nz)
         face = jnp.concatenate([face, face], axis=1).reshape(comps * sx, 1, nz)
         faces_y.append(recv_y[k] + face)
-    smooth(add_faces(r0[...], faces_x, faces_y, 1.0), r0, w_hi, w_lo, ids0, nz // 2, damping)
+    smooth(add_faces(r0[...], faces_x, faces_y, 1.0), r0, w, ids0, nz // 2, damping, block_in, block_out)
     out[...] = permute((x0[...] + r0[...]).reshape(-1, nz), from_lanes).reshape(out.shape)
 
 
@@ -306,11 +324,11 @@
         layers, size, _ = inverses.shape
         cx, cy = sx // 2, sy // 2
         vmem = pl.BlockSpec(memory_space=pltpu.VMEM)
-        smem = pl.BlockSpec(memory_space=pltpu.SMEM)
+        hbm = pl.BlockSpec(memory_space=pltpu.HBM)
         fine, coarse = (comps, sx, sy, nz), (comps, cx, cy, nz)
         scratch = [
-            ((layers * size, size), bf16), ((layers * size, size), bf16),
-            (fine, f32), (fine, f32), (fine, f32), ((sx, sy, nz), f32), ((cx, cy, nz), f32),
+            ((sx // 4 * (sy // 8), size, nz), f32), ((sx // 4 * (sy // 8), size, nz), f32),
+            ((2 * size, layers * size), bf16), (fine, f32), (fine, f32), (fine, f32), ((sx, sy, nz), f32), ((cx, cy, nz), f32),
             (coarse, f32), (coarse, f32), (coarse, f32), (coarse, f32),
         ]
         scratch += [((2, comps, sy, nz), f32)] * 2 + [((2, comps * sx, 1, nz), f32)] * 2
@@ -318,9 +336,12 @@
         return pl.pallas_call(
             functools.partial(kernel, axes, sizes),
             out_shape=jax.ShapeDtypeStruct(source.shape, f32),
-            in_specs=[vmem, vmem, smem, smem, vmem],
+            in_specs=[hbm] * 5,
             out_specs=vmem,
-            scratch_shapes=[pltpu.VMEM(s, t) for s, t in scratch]
+            scratch_shapes=[pltpu.VMEM(source.shape, f32), pltpu.VMEM(cell_class.shape, jnp.int32)]
+            + [pltpu.SMEM(class_conductivity.shape, f32), pltpu.SMEM(layer_of_depth.shape, jnp.int32)]
+            + [pltpu.VMEM(inverses.shape, f32), pltpu.SemaphoreType.DMA((5,))]
+            + [pltpu.VMEM(s, t) for s, t in scratch]
             + [pltpu.SemaphoreType.DMA((3, 4)), pltpu.SemaphoreType.DMA((3, 4))],
             compiler_params=pltpu.CompilerParams(
                 collective_id=0, has_side_effects=True, vmem_limit_bytes=50 * 2**20

time: 26.7 us -> 24.4 us (0.914)
  Pallas kernels: 21.1 us -> 18.9 us
    pallas_call x1, Pallas kernels: 21.1 us -> 18.9 us  [per_device(): pl.pallas_call(functools.partial(kernel, axes, sizes), out_shape=jax.Shap...]
where the time goes in v1:
time: 24.4 us; the launch traced here: 24.2 us
  Pallas kernels  18.9 us (77%)
  local copies, waits for them, and re-layouts  5.3 us (22%)
    pallas_call x1, Pallas kernels, per_device(): pl.pallas_call(functools.partial(kernel, axes, sizes), out_shape=jax.Shap...  18.9 us
    unnamed x11, local copies, waits for them, and re-layouts  5.3 us

profile of v1, /device:TPU:0, one launch (start us, length us, event | category | flops | bytes accessed | tf_op | source)
XLA Modules:
  0.0 24.2 jit_solution(8212455529093958678)
XLA Ops:
  0.0 0.0 copy-start
  0.0 1.4 %copy-done = f32[8,192,192]{2,1,0:T(8,128)S(1)} copy-done((f32[8,192,192]{2,1,0:T(8,128)S(1)}, f32[8,192,192]{2,1,0:T(8,128)}, u32[]{:S(2)}) %copy-start) | copy-done | bytes 1179672
  1.4 0.0 copy-start.1
  1.4 1.0 %copy-done.1 = f32[6,8,16,128]{3,2,1,0:T(8,128)S(1)} copy-done((f32[6,8,16,128]{3,2,1,0:T(8,128)S(1)}, f32[6,8,16,128]{3,2,1,0:T(8,128)}, u32[]{:S(2)}) %copy-start.1) | copy-done | bytes 393240
  2.4 0.0 copy-start.2
  2.4 0.8 %copy-done.2 = s32[8,16,128]{2,1,0:T(8,128)S(1)} copy-done((s32[8,16,128]{2,1,0:T(8,128)S(1)}, s32[8,16,128]{2,1,0:T(8,128)}, u32[]{:S(2)}) %copy-start.2) | copy-done | bytes 65560
  3.2 0.0 copy-start.3
  3.2 0.7 %copy-done.3 = f32[8]{0:T(128)S(1)} copy-done((f32[8]{0:T(128)S(1)}, f32[8]{0:T(128)}, u32[]{:S(2)}) %copy-start.3) | copy-done | bytes 56
  3.9 0.0 copy-start.4
  3.9 0.7 %copy-done.4 = s32[64]{0:T(128)S(1)} copy-done((s32[64]{0:T(128)S(1)}, s32[64]{0:T(128)}, u32[]{:S(2)}) %copy-start.4) | copy-done | bytes 280
  4.6 18.9 %shard_map.55 = f32[6,8,16,128]{3,2,1,0:T(8,128)S(1)} custom-call(f32[6,8,16,128]{3,2,1,0:T(8,128)S(1)} %copy-done.1, s32[8,16,128]{2,1,0:T(8,128)S(1)} %copy-done.2, f32[8]{0:T(128)S(1)} %copy-done.3, s32[64]{0:T(128)S(1)} %copy-done.4, f32[8,192,192]{2,1,0:T(8,128)S(1)} %copy-done), custom_call_target="tpu_custom_call" | custom-call | tf_op jit(solution)/shard_map/pallas_call | solution.py:336
  23.4 0.7 %copy.7 = f32[6,8,16,128]{3,2,1,0:T(8,128)} copy(f32[6,8,16,128]{3,2,1,0:T(8,128)S(1)} %shard_map.55) | data formatting | bytes 786432
Async XLA Ops:
  0.0 1.4 %copy-start = (f32[8,192,192]{2,1,0:T(8,128)S(1)}, f32[8,192,192]{2,1,0:T(8,128)}, u32[]{:S(2)}) copy-start(f32[8,192,192]{2,1,0:T(8,128)} %inv_hbm.1) | copy-start | bytes 3538948
  1.4 1.0 %copy-start.1 = (f32[6,8,16,128]{3,2,1,0:T(8,128)S(1)}, f32[6,8,16,128]{3,2,1,0:T(8,128)}, u32[]{:S(2)}) copy-start(f32[6,8,16,128]{3,2,1,0:T(8,128)} %src_hbm.1) | copy-start | bytes 1179652
  2.4 0.8 %copy-start.2 = (s32[8,16,128]{2,1,0:T(8,128)S(1)}, s32[8,16,128]{2,1,0:T(8,128)}, u32[]{:S(2)}) copy-start(s32[8,16,128]{2,1,0:T(8,128)} %cls_hbm.1) | copy-start | bytes 196612
  3.2 0.7 %copy-start.3 = (f32[8]{0:T(128)S(1)}, f32[8]{0:T(128)}, u32[]{:S(2)}) copy-start(f32[8]{0:T(128)} %cond_hbm.1) | copy-start | bytes 100
  3.9 0.7 %copy-start.4 = (s32[64]{0:T(128)S(1)}, s32[64]{0:T(128)}, u32[]{:S(2)}) copy-start(s32[64]{0:T(128)} %depth_hbm.1) | copy-start | bytes 772

commit v2 on v1

--- a/solution.py
+++ b/solution.py
@@ -36,34 +36,29 @@
     return dot(hi, matrix) + dot(lo, matrix)
 
 
-def pick_rows(x, places):
-    row = iota(x.shape, 1)
-    out = jnp.zeros_like(x)
-    for shift in range(8):
-        rows = [s for s in range(8) if places[s] is not None and (s - places[s]) % 8 == shift]
-        if rows:
-            mask = functools.reduce(jnp.logical_or, [row == s for s in rows])
-            out = jnp.where(mask, roll(x, shift, 1), out)
-    return out
-
-
-def pair_rows(x):
-    tiles = []
-    for t in range(x.shape[1] // 16):
-        low, high = x[:, 16 * t : 16 * t + 8], x[:, 16 * t + 8 : 16 * t + 16]
-        low = low + roll(low, 7, 1)
-        high = high + roll(high, 7, 1)
-        tiles.append(pick_rows(low, [0, 2, 4, 6] + [None] * 4) + pick_rows(high, [None] * 4 + [0, 2, 4, 6]))
-    return jnp.concatenate(tiles, axis=1)
-
-
-def repeat_rows(x):
-    tiles = []
-    for t in range(x.shape[1] // 8):
-        tile = x[:, 8 * t : 8 * t + 8]
-        tiles.append(pick_rows(tile, [0, 0, 1, 1, 2, 2, 3, 3]))
-        tiles.append(pick_rows(tile, [4, 4, 5, 5, 6, 6, 7, 7]))
-    return jnp.concatenate(tiles, axis=1)
+def pair_rows(x, t):
+    n = x.shape[0]
+    t[:n, :] = x
+    return t[pl.ds(0, n // 2, stride=2), :] + t[pl.ds(1, n // 2, stride=2), :]
+
+
+def repeat_rows(x, t):
+    n = x.shape[0]
+    t[pl.ds(0, n, stride=2), :] = x
+    t[pl.ds(1, n, stride=2), :] = x
+    return t[: 2 * n, :]
+
+
+def pack(x):
+    n = x.shape[0] // 2
+    return jnp.where(iota((n,) + x.shape[1:], x.ndim - 1) < x.shape[-1] // 2, x[:n], x[n:])
+
+
+def unpack(x):
+    half = x.shape[-1] // 2
+    turned = roll(x, half, x.ndim - 1)
+    first = iota(x.shape, x.ndim - 1) < half
+    return jnp.concatenate([jnp.where(first, x, turned), jnp.where(first, turned, x)], axis=0)
 
 
 def first_half(shape, half):
@@ -127,39 +122,13 @@
         out_ref[:, 4 * xb : 4 * xb + 4, 8 * p : 8 * p + 8, :] = v
 
 
-def beside_z_fine(u):
-    nz = u.shape[-1]
-    q = nz // 4
-    lane = iota(u.shape, u.ndim - 1)
-    ax = u.ndim - 1
-    other = jnp.where(
-        lane < 2 * q,
-        jnp.where(lane < q, roll(u, q + 1, ax), roll(u, -q, ax)),
-        jnp.where(lane < 3 * q, roll(u, q, ax), roll(u, -q - 1, ax)),
-    )
-    other = jnp.where((lane == 0) | (lane == nz - 1), 0.0, other)
-    return roll(u, 2 * q, ax) + other
-
-
-def beside_z_coarse(u):
-    nz = u.shape[-1]
-    q = nz // 4
-    lane = iota(u.shape, u.ndim - 1)
-    ax = u.ndim - 1
-    mask = first_half(u.shape, q)
-    total = jnp.where(mask, roll(u, -q, ax), roll(u, q, ax))
-    other = jnp.where(mask, roll(u, 1 - q, ax), roll(u, q - 1, ax))
-    edge = (lane == 0) | (lane == 2 * q - 1) | (lane == 2 * q) | (lane == nz - 1)
-    return total + jnp.where(edge, 0.0, other)
-
-
 def residual(b, u, sigma, beside_z, factor):
     comps, sx, sy, nz = u.shape
     half = comps // 2
     flat = u.reshape(comps * sx, sy, nz)
     row = iota(flat.shape, 1)
     near = jnp.where(row == 0, 0.0, roll(flat, 1, 1)) + jnp.where(row == sy - 1, 0.0, roll(flat, -1, 1))
-    near = (near + beside_z(flat)).reshape(u.shape)
+    near = near.reshape(u.shape) + permute(flat.reshape(-1, nz), beside_z).reshape(u.shape)
     zero = jnp.zeros((comps, 1, sy, nz), f32)
     near = near + jnp.concatenate([zero, u[:, :-1]], axis=1) + jnp.concatenate([u[:, 1:], zero], axis=1)
     out = b - (6.0 * u - near) * factor
@@ -178,18 +147,17 @@
     return jnp.concatenate([low, r[:, 1 : sx - 1], high], axis=1)
 
 
-def restrict(u):
+def restrict(u, t):
     comps, sx, sy, nz = u.shape
     v = u.reshape(comps * sx // 2, 2, sy, nz)
-    v = v[:, 0] + v[:, 1]
-    v = pair_rows(v)
-    v = (v + roll(v, nz // 2, 2)) * 0.125
+    v = pair_rows((v[:, 0] + v[:, 1]).reshape(-1, nz), t)
+    v = (v + roll(v, nz // 2, 1)) * 0.125
     return v.reshape(comps, sx // 2, sy // 2, nz)
 
 
 def kernel(
     axes, sizes, src_hbm, cls_hbm, cond_hbm, depth_hbm, inv_hbm, out,
-    src, cls, cond, depth, inv, in_sem, block_in, block_out, w, b0, x0, r0, sig0, sig1, b1, x1, r1, d1,
+    src, cls, cond, depth, inv, in_sem, block_in, block_out, w, b0, x0, r0, sig0, sig1, b1, x1, r1, d1, t,
     send_x, recv_x, send_y, recv_y, csend_x, crecv_x, csend_y, crecv_y, send_sem, recv_sem,
 ):
     comps, sx, sy, nz = src.shape
@@ -216,32 +184,36 @@
                 if ref is recv_x or ref is recv_y:
                     ref[d % 2] = jnp.zeros(ref.shape[1:], f32)
                 else:
-                    for e in range(2):
+                    for e in range(3):
                         ref[e, d % 2] = jnp.zeros(ref.shape[2:], f32)
 
     def copy(e, d):
         if d < 2:
-            s, r = (send_x, recv_x) if e == 0 else (csend_x.at[e - 1], crecv_x.at[e - 1])
+            s, r = (send_x, recv_x) if e == 3 else (csend_x.at[e], crecv_x.at[e])
         else:
-            s, r = (send_y, recv_y) if e == 0 else (csend_y.at[e - 1], crecv_y.at[e - 1])
+            s, r = (send_y, recv_y) if e == 3 else (csend_y.at[e], crecv_y.at[e])
         k = d % 2
         return pltpu.make_async_remote_copy(
             src_ref=s.at[k], dst_ref=r.at[1 - k], send_sem=send_sem.at[e, d], recv_sem=recv_sem.at[e, d ^ 1],
             device_id=device(d), device_id_type=MESH,
         )
 
-    def start(e, u):
-        c, ux, uy, _ = u.shape
-        sxr, syr = (send_x, send_y) if e == 0 else (csend_x.at[e - 1], csend_y.at[e - 1])
-        sxr[0] = u[:, 0]
-        sxr[1] = u[:, ux - 1]
-        flat = u.reshape(c * ux, uy, nz)
-        syr[0] = flat[:, 0:1]
-        syr[1] = flat[:, uy - 1 : uy]
+    def launch(e):
         for d in range(4):
             @pl.when(has[d])
             def _(d=d):
                 copy(e, d).start()
+
+    def start(e, u):
+        c, ux, uy, _ = u.shape
+        flat = u.reshape(c * ux, uy, nz)
+        for k in range(2):
+            csend_x[e, k] = pack(u[:, k * (ux - 1)])
+            csend_y[e, k] = pack(flat[:, k * (uy - 1) : k * (uy - 1) + 1])
+        launch(e)
+
+    def faces(e):
+        return [unpack(crecv_x[e, k]) for k in range(2)], [unpack(crecv_y[e, k]) for k in range(2)]
 
     def finish(e):
         for d in range(4):
@@ -258,6 +230,12 @@
         return 4 * (rest - q * zic) + 2 * zic + zi
     to_lanes = jnp.where(iota((nz, nz), 0) == z_of(iota((nz, nz), 1)), 1.0, 0.0).astype(bf16)
     from_lanes = jnp.where(iota((nz, nz), 1) == z_of(iota((nz, nz), 0)), 1.0, 0.0).astype(bf16)
+
+    beside0 = jnp.where(jnp.abs(z_of(iota((nz, nz), 0)) - z_of(iota((nz, nz), 1))) == 1, 1.0, 0.0).astype(bf16)
+    def zc_of(lane):
+        return z_of(lane - jnp.where(lane >= 2 * q, 2 * q, 0)) // 2
+    near1 = jnp.abs(zc_of(iota((nz, nz), 0)) - zc_of(iota((nz, nz), 1))) == 1
+    beside1 = jnp.where(near1 & (iota((nz, nz), 0) < 2 * q), 1.0, 0.0).astype(bf16)
 
     loads[0].wait()
     b0[...] = permute(src[...].reshape(-1, nz), to_lanes).reshape(src.shape)
@@ -269,11 +247,11 @@
         sigma = jnp.where(kinds == float(k), cond[k], sigma)
     sigma = sigma.reshape(sx, sy, nz)
     sig0[...] = sigma
-    sig1[...] = restrict(sigma[None])[0]
+    sig1[...] = restrict(sigma[None], t)[0]
 
     loads[3].wait()
     lane = iota((1, nz), 1)
-    zb = z_of(lane - jnp.where(lane >= 2 * q, 2 * q, 0)) // 2
+    zb = zc_of(lane)
     ids0 = jnp.zeros((1, nz), jnp.int32)
     for k in range(depth.shape[0]):
         ids0 = jnp.where(zb == k, depth[k], ids0)
@@ -287,30 +265,42 @@
 
     smooth(b0[...], x0, w, ids0, nz // 2, damping, block_in, block_out)
     pl.semaphore_wait(barrier, sum(jnp.where(h, 1, 0) for h in has))
-    start(0, x0[...])
-    r0[...] = residual(b0[...], x0[...], sig0[...], beside_z_fine, 1.0)
+    flat = x0[...].reshape(comps * sx, sy, nz)
+    for k in range(2):
+        face = x0[:, k * (sx - 1)]
+        face = pair_rows(face.reshape(comps * sy, nz), t).reshape(comps, sy // 2, nz)
+        csend_x[0, k] = pack((face + roll(face, nz // 2, 2)) * 0.125)
+        send_y[k] = flat[:, k * (sy - 1) : k * (sy - 1) + 1]
+        face = send_y[k].reshape(comps * sx // 2, 2, 1, nz)
+        face = face[:, 0] + face[:, 1]
+        csend_y[0, k] = pack((face + roll(face, nz // 2, 2)) * 0.125)
+        send_x[k] = x0[:, k * (sx - 1)]
+    launch(0)
+    r0[...] = residual(b0[...], x0[...], sig0[...], beside0, 1.0)
+    b1[...] = restrict(r0[...], t)
     finish(0)
-    b1[...] = restrict(add_faces(r0[...], recv_x, recv_y, 1.0))
+    launch(3)
+    b1[...] = add_faces(b1[...], *faces(0), 1.0)
 
     smooth(b1[...], x1, w, ids1, q, damping * 4.0, block_in, block_out)
     start(1, x1[...])
-    r1[...] = residual(b1[...], x1[...], sig1[...], beside_z_coarse, 0.25)
+    r1[...] = residual(b1[...], x1[...], sig1[...], beside1, 0.25)
     finish(1)
-    smooth(add_faces(r1[...], crecv_x.at[0], crecv_y.at[0], 0.25), d1, w, ids1, q, damping * 4.0, block_in, block_out)
+    smooth(add_faces(r1[...], *faces(1), 0.25), d1, w, ids1, q, damping * 4.0, block_in, block_out)
     xc = x1[...] + d1[...]
     start(2, xc)
     cx, cy = sx // 2, sy // 2
-    spread = repeat_rows(xc.reshape(comps * cx, cy, nz)).reshape(comps, cx, 1, sy, nz)
+    spread = repeat_rows(xc.reshape(-1, nz), t).reshape(comps, cx, 1, sy, nz)
     spread = jnp.concatenate([spread, spread], axis=2).reshape(src.shape)
     x0[...] = x0[...] + spread
-    r0[...] = residual(b0[...], x0[...], sig0[...], beside_z_fine, 1.0)
+    r0[...] = residual(b0[...], x0[...], sig0[...], beside0, 1.0)
+    finish(3)
     finish(2)
-    faces_x = [recv_x[k] + repeat_rows(crecv_x[1, k]) for k in range(2)]
-    faces_y = []
+    faces_x, faces_y = faces(2)
     for k in range(2):
-        face = crecv_y[1, k].reshape(comps * cx, 1, 1, nz)
-        face = jnp.concatenate([face, face], axis=1).reshape(comps * sx, 1, nz)
-        faces_y.append(recv_y[k] + face)
+        faces_x[k] = recv_x[k] + repeat_rows(faces_x[k].reshape(-1, nz), t).reshape(comps, sy, nz)
+        face = faces_y[k].reshape(comps * cx, 1, 1, nz)
+        faces_y[k] = recv_y[k] + jnp.concatenate([face, face], axis=1).reshape(comps * sx, 1, nz)
     smooth(add_faces(r0[...], faces_x, faces_y, 1.0), r0, w, ids0, nz // 2, damping, block_in, block_out)
     out[...] = permute((x0[...] + r0[...]).reshape(-1, nz), from_lanes).reshape(out.shape)
 
@@ -329,10 +319,10 @@
         scratch = [
             ((sx // 4 * (sy // 8), size, nz), f32), ((sx // 4 * (sy // 8), size, nz), f32),
             ((2 * size, layers * size), bf16), (fine, f32), (fine, f32), (fine, f32), ((sx, sy, nz), f32), ((cx, cy, nz), f32),
-            (coarse, f32), (coarse, f32), (coarse, f32), (coarse, f32),
+            (coarse, f32), (coarse, f32), (coarse, f32), (coarse, f32), ((comps * cx * sy, nz), f32),
         ]
         scratch += [((2, comps, sy, nz), f32)] * 2 + [((2, comps * sx, 1, nz), f32)] * 2
-        scratch += [((2, 2, comps, cy, nz), f32)] * 2 + [((2, 2, comps * cx, 1, nz), f32)] * 2
+        scratch += [((3, 2, comps // 2, cy, nz), f32)] * 2 + [((3, 2, comps * cx // 2, 1, nz), f32)] * 2
         return pl.pallas_call(
             functools.partial(kernel, axes, sizes),
             out_shape=jax.ShapeDtypeStruct(source.shape, f32),
@@ -342,9 +332,9 @@
             + [pltpu.SMEM(class_conductivity.shape, f32), pltpu.SMEM(layer_of_depth.shape, jnp.int32)]
             + [pltpu.VMEM(inverses.shape, f32), pltpu.SemaphoreType.DMA((5,))]
             + [pltpu.VMEM(s, t) for s, t in scratch]
-            + [pltpu.SemaphoreType.DMA((3, 4)), pltpu.SemaphoreType.DMA((3, 4))],
+            + [pltpu.SemaphoreType.DMA((4, 4)), pltpu.SemaphoreType.DMA((4, 4))],
             compiler_params=pltpu.CompilerParams(
-                collective_id=0, has_side_effects=True, vmem_limit_bytes=50 * 2**20
+                collective_id=0, has_side_effects=True, vmem_limit_bytes=64 * 2**20
             ),
         )(source, cell_class, class_conductivity, layer_of_depth, inverses)
 

time: 24.4 us -> 21.1 us (0.86)
  local copies, waits for them, and re-layouts: 5.3 us -> 1.78 us
    unnamed x11 -> x1, local copies, waits for them, and re-layouts: 5.3 us -> 1.78 us
    pallas_call x1, Pallas kernels: 18.9 us -> 19.1 us  [per_device(): pl.pallas_call(functools.partial(kernel, axes, sizes), out_shape=jax.Shap...]
where the time goes in v2:
time: 21.1 us; the launch traced here: 20.9 us
  Pallas kernels  19.1 us (91%)
  local copies, waits for them, and re-layouts  1.78 us (8%)
    pallas_call x1, Pallas kernels, per_device(): pl.pallas_call(functools.partial(kernel, axes, sizes), out_shape=jax.Shap...  19.1 us
    unnamed x1, local copies, waits for them, and re-layouts  1.78 us

profile of v2, /device:TPU:0, one launch (start us, length us, event | category | flops | bytes accessed | tf_op | source)
XLA Modules:
  0.0 20.9 jit_solution(6884087503469007426)
XLA Ops:
  0.0 19.1 %shard_map.55 = f32[6,8,16,128]{3,2,1,0:T(8,128)} custom-call(f32[6,8,16,128]{3,2,1,0:T(8,128)} %src_hbm.1, s32[8,16,128]{2,1,0:T(8,128)} %cls_hbm.1, f32[8]{0:T(128)} %cond_hbm.1, s32[64]{0:T(128)} %depth_hbm.1, f32[8,192,192]{2,1,0:T(8,128)} %inv_hbm.1), custom_call_target="tpu_custom_call" | custom-call | tf_op jit(solution)/shard_map/pallas_call | solution.py:326
  19.1 1.8 %copy.7 = f32[6,8,16,128]{3,2,1,0:T(8,128)} copy(f32[6,8,16,128]{3,2,1,0:T(8,128)} %shard_map.55) | data formatting | bytes 786432

commit v3 on v2

--- a/solution.py
+++ b/solution.py
@@ -198,8 +198,8 @@
             device_id=device(d), device_id_type=MESH,
         )
 
-    def launch(e):
-        for d in range(4):
+    def launch(e, directions=range(4)):
+        for d in directions:
             @pl.when(has[d])
             def _(d=d):
                 copy(e, d).start()
@@ -209,8 +209,10 @@
         flat = u.reshape(c * ux, uy, nz)
         for k in range(2):
             csend_x[e, k] = pack(u[:, k * (ux - 1)])
+        launch(e, (0, 1))
+        for k in range(2):
             csend_y[e, k] = pack(flat[:, k * (uy - 1) : k * (uy - 1) + 1])
-        launch(e)
+        launch(e, (2, 3))
 
     def faces(e):
         return [unpack(crecv_x[e, k]) for k in range(2)], [unpack(crecv_y[e, k]) for k in range(2)]
@@ -220,7 +222,6 @@
             @pl.when(has[d])
             def _(d=d):
                 copy(e, d ^ 1).wait_recv()
-                copy(e, d).wait_send()
 
     q = nz // 4
     def z_of(lane):
@@ -239,6 +240,36 @@
 
     loads[0].wait()
     b0[...] = permute(src[...].reshape(-1, nz), to_lanes).reshape(src.shape)
+
+    loads[3].wait()
+    lane = iota((1, nz), 1)
+    zb = zc_of(lane)
+    ids0 = jnp.zeros((1, nz), jnp.int32)
+    for k in range(depth.shape[0]):
+        ids0 = jnp.where(zb == k, depth[k], ids0)
+    ids1 = jnp.where(first_half((1, nz), q), ids0, roll(ids0, q, 1))
+
+    loads[4].wait()
+    layers, size, _ = inv.shape
+    hi, lo = split(jnp.concatenate([inv[layer] for layer in range(layers)], axis=1))
+    w[:size, :] = hi
+    w[size:, :] = lo
+
+    smooth(b0[...], x0, w, ids0, nz // 2, damping, block_in, block_out)
+    pl.semaphore_wait(barrier, sum(jnp.where(h, 1, 0) for h in has))
+    flat = x0[...].reshape(comps * sx, sy, nz)
+    for k in range(2):
+        face = x0[:, k * (sx - 1)]
+        face = pair_rows(face.reshape(comps * sy, nz), t).reshape(comps, sy // 2, nz)
+        csend_x[0, k] = pack((face + roll(face, nz // 2, 2)) * 0.125)
+    launch(0, (0, 1))
+    for k in range(2):
+        send_y[k] = flat[:, k * (sy - 1) : k * (sy - 1) + 1]
+        face = send_y[k].reshape(comps * sx // 2, 2, 1, nz)
+        face = face[:, 0] + face[:, 1]
+        csend_y[0, k] = pack((face + roll(face, nz // 2, 2)) * 0.125)
+    launch(0, (2, 3))
+
     loads[1].wait()
     kinds = dot(cls[...].reshape(-1, nz).astype(f32).astype(bf16), to_lanes)
     loads[2].wait()
@@ -249,37 +280,12 @@
     sig0[...] = sigma
     sig1[...] = restrict(sigma[None], t)[0]
 
-    loads[3].wait()
-    lane = iota((1, nz), 1)
-    zb = zc_of(lane)
-    ids0 = jnp.zeros((1, nz), jnp.int32)
-    for k in range(depth.shape[0]):
-        ids0 = jnp.where(zb == k, depth[k], ids0)
-    ids1 = jnp.where(first_half((1, nz), q), ids0, roll(ids0, q, 1))
-
-    loads[4].wait()
-    layers, size, _ = inv.shape
-    hi, lo = split(jnp.concatenate([inv[layer] for layer in range(layers)], axis=1))
-    w[:size, :] = hi
-    w[size:, :] = lo
-
-    smooth(b0[...], x0, w, ids0, nz // 2, damping, block_in, block_out)
-    pl.semaphore_wait(barrier, sum(jnp.where(h, 1, 0) for h in has))
-    flat = x0[...].reshape(comps * sx, sy, nz)
+    r0[...] = residual(b0[...], x0[...], sig0[...], beside0, 1.0)
     for k in range(2):
-        face = x0[:, k * (sx - 1)]
-        face = pair_rows(face.reshape(comps * sy, nz), t).reshape(comps, sy // 2, nz)
-        csend_x[0, k] = pack((face + roll(face, nz // 2, 2)) * 0.125)
-        send_y[k] = flat[:, k * (sy - 1) : k * (sy - 1) + 1]
-        face = send_y[k].reshape(comps * sx // 2, 2, 1, nz)
-        face = face[:, 0] + face[:, 1]
-        csend_y[0, k] = pack((face + roll(face, nz // 2, 2)) * 0.125)
         send_x[k] = x0[:, k * (sx - 1)]
-    launch(0)
-    r0[...] = residual(b0[...], x0[...], sig0[...], beside0, 1.0)
+    launch(3)
     b1[...] = restrict(r0[...], t)
     finish(0)
-    launch(3)
     b1[...] = add_faces(b1[...], *faces(0), 1.0)
 
     smooth(b1[...], x1, w, ids1, q, damping * 4.0, block_in, block_out)
@@ -303,6 +309,11 @@
         faces_y[k] = recv_y[k] + jnp.concatenate([face, face], axis=1).reshape(comps * sx, 1, nz)
     smooth(add_faces(r0[...], faces_x, faces_y, 1.0), r0, w, ids0, nz // 2, damping, block_in, block_out)
     out[...] = permute((x0[...] + r0[...]).reshape(-1, nz), from_lanes).reshape(out.shape)
+    for e in range(4):
+        for d in range(4):
+            @pl.when(has[d])
+            def _(e=e, d=d):
+                copy(e, d).wait_send()
 
 
 def solution(mesh):
@@ -310,6 +321,7 @@
     sizes = tuple(mesh.shape[a] for a in axes)
 
     def per_device(source, cell_class, class_conductivity, layer_of_depth, inverses):
+        operands = (source, cell_class, class_conductivity, layer_of_depth, inverses)
         comps, sx, sy, nz = source.shape
         layers, size, _ = inverses.shape
         cx, cy = sx // 2, sy // 2
@@ -334,9 +346,9 @@
             + [pltpu.VMEM(s, t) for s, t in scratch]
             + [pltpu.SemaphoreType.DMA((4, 4)), pltpu.SemaphoreType.DMA((4, 4))],
             compiler_params=pltpu.CompilerParams(
-                collective_id=0, has_side_effects=True, vmem_limit_bytes=64 * 2**20
+                collective_id=0, has_side_effects=True, vmem_limit_bytes=50 * 2**20
             ),
-        )(source, cell_class, class_conductivity, layer_of_depth, inverses)
+        )(*(pltpu.with_memory_space_constraint(v, pltpu.HBM) for v in operands))
 
     return jax.shard_map(
         per_device,

time: 21.1 us -> 20.1 us (0.953)
  local copies, waits for them, and re-layouts: 1.78 us -> 0.75 us
    unnamed x1, local copies, waits for them, and re-layouts: 1.78 us -> 0.75 us
where the time goes in v3:
time: 20.1 us; the launch traced here: 20 us
  Pallas kernels  19.2 us (96%)
  local copies, waits for them, and re-layouts  0.75 us (4%)
    pallas_call x1, Pallas kernels, per_device(): pl.pallas_call(functools.partial(kernel, axes, sizes), out_shape=jax.Shap...  19.2 us
    unnamed x1, local copies, waits for them, and re-layouts  0.75 us

profile of v3, /device:TPU:0, one launch (start us, length us, event | category | flops | bytes accessed | tf_op | source)
XLA Modules:
  0.0 20.0 jit_solution(16897743413722840047)
XLA Ops:
  0.0 19.2 %shard_map.55 = f32[6,8,16,128]{3,2,1,0:T(8,128)S(1)} custom-call(f32[6,8,16,128]{3,2,1,0:T(8,128)} %src_hbm.1, s32[8,16,128]{2,1,0:T(8,128)} %cls_hbm.1, f32[8]{0:T(128)} %cond_hbm.1, s32[64]{0:T(128)} %depth_hbm.1, f32[8,192,192]{2,1,0:T(8,128)} %inv_hbm.1), custom_call_target="tpu_custom_call" | custom-call | tf_op jit(solution)/shard_map/pallas_call | solution.py:338
  19.2 0.7 %copy.7 = f32[6,8,16,128]{3,2,1,0:T(8,128)} copy(f32[6,8,16,128]{3,2,1,0:T(8,128)S(1)} %shard_map.55) | data formatting | bytes 786432

commit v4 on v3

--- a/solution.py
+++ b/solution.py
@@ -88,7 +88,7 @@
     return jnp.concatenate(out, axis=0)
 
 
-def smooth(field, out_ref, w, ids, half, scale, block_in, block_out):
+def smooth(field, out_ref, w, ids, half, scale, block_in, block_out, mix_in=None, mix_out=None):
     comps, sx, sy, nz = field.shape
     rows = comps * 16
     size = 2 * rows
@@ -97,7 +97,12 @@
     for at, (xb, p) in enumerate(pairs):
         v = field[:, 4 * xb : 4 * xb + 4, 8 * p : 8 * p + 8, :].reshape(comps * 2, 2, 8, nz)
         u0, u1 = swap_tiles(v[:, 0], v[:, 1])
-        even, odd = swap_lanes(u0.reshape(rows, nz), u1.reshape(rows, nz), half)
+        u0, u1 = u0.reshape(rows, nz), u1.reshape(rows, nz)
+        if mix_in is None:
+            even, odd = swap_lanes(u0, u1, half)
+        else:
+            mixed = permute(jnp.concatenate([u0, u1], axis=1), mix_in)
+            even, odd = mixed[:, :nz], mixed[:, nz:]
         block_in[at, pl.ds(0, rows, stride=2), :] = even
         block_in[at, pl.ds(1, rows, stride=2), :] = odd
     n = len(pairs) * nz
@@ -116,10 +121,15 @@
         block_out[at] = total[:, at * nz : (at + 1) * nz]
         even = block_out[at, pl.ds(0, rows, stride=2), :]
         odd = block_out[at, pl.ds(1, rows, stride=2), :]
-        u0, u1 = swap_lanes(even, odd, half)
+        if mix_out is None:
+            u0, u1 = swap_lanes(even, odd, half)
+        else:
+            mixed = permute(jnp.concatenate([even, odd], axis=1), mix_out)
+            u0, u1 = mixed[:, :nz], mixed[:, nz:]
         v0, v1 = swap_tiles(u0.reshape(comps * 2, 8, nz), u1.reshape(comps * 2, 8, nz))
         v = jnp.stack([v0, v1], axis=1).reshape(comps, 4, 8, nz)
-        out_ref[:, 4 * xb : 4 * xb + 4, 8 * p : 8 * p + 8, :] = v
+        at = (slice(None), slice(4 * xb, 4 * xb + 4), slice(8 * p, 8 * p + 8), slice(None))
+        out_ref[at] = v if mix_out is None else out_ref[at] + v
 
 
 def residual(b, u, sigma, beside_z, factor):
@@ -181,17 +191,17 @@
         @pl.when(jnp.logical_not(has[d]))
         def _(d=d):
             for ref in [(recv_x, crecv_x), (recv_y, crecv_y)][d // 2]:
-                if ref is recv_x or ref is recv_y:
+                if ref is recv_y:
                     ref[d % 2] = jnp.zeros(ref.shape[1:], f32)
                 else:
-                    for e in range(3):
+                    for e in range(ref.shape[0]):
                         ref[e, d % 2] = jnp.zeros(ref.shape[2:], f32)
 
     def copy(e, d):
         if d < 2:
-            s, r = (send_x, recv_x) if e == 3 else (csend_x.at[e], crecv_x.at[e])
+            s, r = (send_x.at[e - 3], recv_x.at[e - 3]) if e >= 3 else (csend_x.at[e], crecv_x.at[e])
         else:
-            s, r = (send_y, recv_y) if e == 3 else (csend_y.at[e], crecv_y.at[e])
+            s, r = (send_y, recv_y) if e >= 3 else (csend_y.at[e], crecv_y.at[e])
         k = d % 2
         return pltpu.make_async_remote_copy(
             src_ref=s.at[k], dst_ref=r.at[1 - k], send_sem=send_sem.at[e, d], recv_sem=recv_sem.at[e, d ^ 1],
@@ -217,8 +227,8 @@
     def faces(e):
         return [unpack(crecv_x[e, k]) for k in range(2)], [unpack(crecv_y[e, k]) for k in range(2)]
 
-    def finish(e):
-        for d in range(4):
+    def finish(e, directions=range(4)):
+        for d in directions:
             @pl.when(has[d])
             def _(d=d):
                 copy(e, d ^ 1).wait_recv()
@@ -238,10 +248,9 @@
     near1 = jnp.abs(zc_of(iota((nz, nz), 0)) - zc_of(iota((nz, nz), 1))) == 1
     beside1 = jnp.where(near1 & (iota((nz, nz), 0) < 2 * q), 1.0, 0.0).astype(bf16)
 
-    loads[0].wait()
-    b0[...] = permute(src[...].reshape(-1, nz), to_lanes).reshape(src.shape)
-
-    loads[3].wait()
+    for i in (0, 3, 4):
+        loads[i].wait()
+
     lane = iota((1, nz), 1)
     zb = zc_of(lane)
     ids0 = jnp.zeros((1, nz), jnp.int32)
@@ -249,13 +258,20 @@
         ids0 = jnp.where(zb == k, depth[k], ids0)
     ids1 = jnp.where(first_half((1, nz), q), ids0, roll(ids0, q, 1))
 
-    loads[4].wait()
     layers, size, _ = inv.shape
     hi, lo = split(jnp.concatenate([inv[layer] for layer in range(layers)], axis=1))
     w[:size, :] = hi
     w[size:, :] = lo
 
-    smooth(b0[...], x0, w, ids0, nz // 2, damping, block_in, block_out)
+    def mix(a, b):
+        side = jnp.where(b >= nz, 1, 0)
+        lane = b - nz * side
+        second = jnp.where(lane >= 2 * q, 1, 0)
+        return jnp.where(a == nz * second + z_of(lane - 2 * q * second + 2 * q * side), 1.0, 0.0).astype(bf16)
+    wide = (2 * nz, 2 * nz)
+    mix_in, mix_out = mix(iota(wide, 0), iota(wide, 1)), mix(iota(wide, 1), iota(wide, 0))
+
+    smooth(src[...], x0, w, ids0, nz // 2, damping, block_in, block_out, mix_in=mix_in)
     pl.semaphore_wait(barrier, sum(jnp.where(h, 1, 0) for h in has))
     flat = x0[...].reshape(comps * sx, sy, nz)
     for k in range(2):
@@ -280,18 +296,21 @@
     sig0[...] = sigma
     sig1[...] = restrict(sigma[None], t)[0]
 
+    b0[...] = permute(src[...].reshape(-1, nz), to_lanes).reshape(src.shape)
     r0[...] = residual(b0[...], x0[...], sig0[...], beside0, 1.0)
     for k in range(2):
-        send_x[k] = x0[:, k * (sx - 1)]
-    launch(3)
+        for h in range(2):
+            send_x[h, k] = x0[h * (comps // 2) : (h + 1) * (comps // 2), k * (sx - 1)]
     b1[...] = restrict(r0[...], t)
     finish(0)
+    launch(3)
     b1[...] = add_faces(b1[...], *faces(0), 1.0)
 
     smooth(b1[...], x1, w, ids1, q, damping * 4.0, block_in, block_out)
     start(1, x1[...])
     r1[...] = residual(b1[...], x1[...], sig1[...], beside1, 0.25)
     finish(1)
+    launch(4, (0, 1))
     smooth(add_faces(r1[...], *faces(1), 0.25), d1, w, ids1, q, damping * 4.0, block_in, block_out)
     xc = x1[...] + d1[...]
     start(2, xc)
@@ -300,17 +319,20 @@
     spread = jnp.concatenate([spread, spread], axis=2).reshape(src.shape)
     x0[...] = x0[...] + spread
     r0[...] = residual(b0[...], x0[...], sig0[...], beside0, 1.0)
+    out[...] = permute(x0[...].reshape(-1, nz), from_lanes).reshape(out.shape)
     finish(3)
+    finish(4, (0, 1))
     finish(2)
     faces_x, faces_y = faces(2)
     for k in range(2):
-        faces_x[k] = recv_x[k] + repeat_rows(faces_x[k].reshape(-1, nz), t).reshape(comps, sy, nz)
+        faces_x[k] = jnp.concatenate([recv_x[0, k], recv_x[1, k]], axis=0) + repeat_rows(faces_x[k].reshape(-1, nz), t).reshape(comps, sy, nz)
         face = faces_y[k].reshape(comps * cx, 1, 1, nz)
         faces_y[k] = recv_y[k] + jnp.concatenate([face, face], axis=1).reshape(comps * sx, 1, nz)
-    smooth(add_faces(r0[...], faces_x, faces_y, 1.0), r0, w, ids0, nz // 2, damping, block_in, block_out)
-    out[...] = permute((x0[...] + r0[...]).reshape(-1, nz), from_lanes).reshape(out.shape)
-    for e in range(4):
-        for d in range(4):
+    smooth(
+        add_faces(r0[...], faces_x, faces_y, 1.0), out, w, ids0, nz // 2, damping, block_in, block_out, mix_out=mix_out
+    )
+    for e in range(5):
+        for d in range(4 if e < 4 else 2):
             @pl.when(has[d])
             def _(e=e, d=d):
                 copy(e, d).wait_send()
@@ -333,7 +355,7 @@
             ((2 * size, layers * size), bf16), (fine, f32), (fine, f32), (fine, f32), ((sx, sy, nz), f32), ((cx, cy, nz), f32),
             (coarse, f32), (coarse, f32), (coarse, f32), (coarse, f32), ((comps * cx * sy, nz), f32),
         ]
-        scratch += [((2, comps, sy, nz), f32)] * 2 + [((2, comps * sx, 1, nz), f32)] * 2
+        scratch += [((2, 2, comps // 2, sy, nz), f32)] * 2 + [((2, comps * sx, 1, nz), f32)] * 2
         scratch += [((3, 2, comps // 2, cy, nz), f32)] * 2 + [((3, 2, comps * cx // 2, 1, nz), f32)] * 2
         return pl.pallas_call(
             functools.partial(kernel, axes, sizes),
@@ -344,7 +366,7 @@
             + [pltpu.SMEM(class_conductivity.shape, f32), pltpu.SMEM(layer_of_depth.shape, jnp.int32)]
             + [pltpu.VMEM(inverses.shape, f32), pltpu.SemaphoreType.DMA((5,))]
             + [pltpu.VMEM(s, t) for s, t in scratch]
-            + [pltpu.SemaphoreType.DMA((4, 4)), pltpu.SemaphoreType.DMA((4, 4))],
+            + [pltpu.SemaphoreType.DMA((5, 4)), pltpu.SemaphoreType.DMA((5, 4))],
             compiler_params=pltpu.CompilerParams(
                 collective_id=0, has_side_effects=True, vmem_limit_bytes=50 * 2**20
             ),

time: 20.1 us -> 19.2 us (0.955)
  Pallas kernels: 19.2 us -> 18.3 us
    pallas_call x1, Pallas kernels: 19.2 us -> 18.3 us  [per_device(): pl.pallas_call(functools.partial(kernel, axes, sizes), out_shape=jax.Shap...]
where the time goes in v4:
time: 19.2 us; the launch traced here: 19.1 us
  Pallas kernels  18.3 us (95%)
  local copies, waits for them, and re-layouts  0.75 us (4%)
    pallas_call x1, Pallas kernels, per_device(): pl.pallas_call(functools.partial(kernel, axes, sizes), out_shape=jax.Shap...  18.3 us
    unnamed x1, local copies, waits for them, and re-layouts  0.75 us

profile of v4, /device:TPU:0, one launch (start us, length us, event | category | flops | bytes accessed | tf_op | source)
XLA Modules:
  0.0 19.1 jit_solution(8677658604639881497)
XLA Ops:
  0.0 18.3 %shard_map.55 = f32[6,8,16,128]{3,2,1,0:T(8,128)S(1)} custom-call(f32[6,8,16,128]{3,2,1,0:T(8,128)} %src_hbm.1, s32[8,16,128]{2,1,0:T(8,128)} %cls_hbm.1, f32[8]{0:T(128)} %cond_hbm.1, s32[64]{0:T(128)} %depth_hbm.1, f32[8,192,192]{2,1,0:T(8,128)} %inv_hbm.1), custom_call_target="tpu_custom_call" | custom-call | tf_op jit(solution)/shard_map/pallas_call | solution.py:360
  18.3 0.7 %copy.7 = f32[6,8,16,128]{3,2,1,0:T(8,128)} copy(f32[6,8,16,128]{3,2,1,0:T(8,128)S(1)} %shard_map.55) | data formatting | bytes 786432

commit v5 on v4

--- a/solution.py
+++ b/solution.py
@@ -105,20 +105,21 @@
             even, odd = mixed[:, :nz], mixed[:, nz:]
         block_in[at, pl.ds(0, rows, stride=2), :] = even
         block_in[at, pl.ds(1, rows, stride=2), :] = odd
-    n = len(pairs) * nz
-    hi, lo = split(jnp.concatenate([block_in[at] for at in range(len(pairs))], axis=1))
+    x = jnp.concatenate([block_in[at, :size, :] for at in range(len(pairs))], axis=1)
+    hi, lo = split(x)
     ids = jnp.concatenate([ids] * len(pairs), axis=1)
-    if n < 256:
-        x = masked(jnp.concatenate([hi, lo], axis=1), jnp.concatenate([ids, ids], axis=1), layers)
-        total = dot(w[...], x)
+    twice = half < nz // 2
+    if twice:
+        x = jnp.where(first_half(x.shape, nz // 2), hi.astype(f32), x - hi.astype(f32)).astype(bf16)
+        total = dot(w[...], masked(x, ids, layers))
         total = total[:size] + total[size:]
-        total = total[:, :n] + total[:, n:]
     else:
         total = dot(w[...], masked(hi, ids, layers))
         total = total[:size] + total[size:] + dot(w[:size, :], masked(lo, ids, layers))
     total = total * scale
     for at, (xb, p) in enumerate(pairs):
-        block_out[at] = total[:, at * nz : (at + 1) * nz]
+        block = total[:, at * nz : (at + 1) * nz]
+        block_out[at, :size, :] = block + roll(block, nz // 2, 1) if twice else block
         even = block_out[at, pl.ds(0, rows, stride=2), :]
         odd = block_out[at, pl.ds(1, rows, stride=2), :]
         if mix_out is None:
@@ -128,8 +129,13 @@
             u0, u1 = mixed[:, :nz], mixed[:, nz:]
         v0, v1 = swap_tiles(u0.reshape(comps * 2, 8, nz), u1.reshape(comps * 2, 8, nz))
         v = jnp.stack([v0, v1], axis=1).reshape(comps, 4, 8, nz)
-        at = (slice(None), slice(4 * xb, 4 * xb + 4), slice(8 * p, 8 * p + 8), slice(None))
-        out_ref[at] = v if mix_out is None else out_ref[at] + v
+        if mix_out is None:
+            for c in range(comps):
+                for i in range(4):
+                    out_ref[pl.ds((c * sx + 4 * xb + i) * sy + 8 * p, 8), :] = v[c, i]
+        else:
+            at = (slice(None), slice(4 * xb, 4 * xb + 4), slice(8 * p, 8 * p + 8), slice(None))
+            out_ref[at] = out_ref[at] + v
 
 
 def residual(b, u, sigma, beside_z, factor):
@@ -146,15 +152,14 @@
     return out + turned
 
 
-def add_faces(r, faces_x, faces_y, factor):
-    comps, sx, sy, nz = r.shape
-    row = iota((comps * sx, sy, nz), 1)
-    flat = r.reshape(comps * sx, sy, nz)
-    flat = flat + jnp.where(row == 0, faces_y[0] * factor, 0.0) + jnp.where(row == sy - 1, faces_y[1] * factor, 0.0)
-    r = flat.reshape(r.shape)
-    low = r[:, :1] + faces_x[0][:, None] * factor
-    high = r[:, sx - 1 :] + faces_x[1][:, None] * factor
-    return jnp.concatenate([low, r[:, 1 : sx - 1], high], axis=1)
+def add_faces(r, shape, faces_x, faces_y):
+    comps, sx, sy, nz = shape
+    for k in range(2):
+        for c in range(comps):
+            at = pl.ds((c * sx + k * (sx - 1)) * sy, sy)
+            r[at, :] = r[at, :] + faces_x[k][c]
+        at = pl.ds(k * (sy - 1), comps * sx, stride=sy)
+        r[at, :] = r[at, :] + faces_y[k]
 
 
 def restrict(u, t):
@@ -171,7 +176,9 @@
     send_x, recv_x, send_y, recv_y, csend_x, crecv_x, csend_y, crecv_y, send_sem, recv_sem,
 ):
     comps, sx, sy, nz = src.shape
-    named = ((src_hbm, src), (cls_hbm, cls), (cond_hbm, cond), (depth_hbm, depth), (inv_hbm, inv))
+    named = ((src_hbm, src), (cls_hbm, cls), (cond_hbm, cond), (depth_hbm, depth))
+    layers, size, _ = inv.shape
+    named += tuple((inv_hbm.at[layer], inv.at[layer]) for layer in range(layers))
     loads = [pltpu.make_async_copy(a, b, in_sem.at[i]) for i, (a, b) in enumerate(named)]
     for load in loads:
         load.start()
@@ -214,18 +221,20 @@
             def _(d=d):
                 copy(e, d).start()
 
+    fine, coarse = src.shape, (comps, sx // 2, sy // 2, nz)
+    nf, nc = comps * sx * sy, comps * (sx // 2) * (sy // 2)
+
     def start(e, u):
-        c, ux, uy, _ = u.shape
-        flat = u.reshape(c * ux, uy, nz)
+        _, ux, uy, _ = coarse
         for k in range(2):
-            csend_x[e, k] = pack(u[:, k * (ux - 1)])
+            csend_x[e, k] = pack(u[:nc, :].reshape(coarse)[:, k * (ux - 1)])
         launch(e, (0, 1))
         for k in range(2):
-            csend_y[e, k] = pack(flat[:, k * (uy - 1) : k * (uy - 1) + 1])
+            csend_y[e, k] = u[pl.ds(k * (uy - 1), comps * ux, stride=uy), :]
         launch(e, (2, 3))
 
-    def faces(e):
-        return [unpack(crecv_x[e, k]) for k in range(2)], [unpack(crecv_y[e, k]) for k in range(2)]
+    def faces(e, factor):
+        return [unpack(crecv_x[e, k]) * factor for k in range(2)], [crecv_y[e, k] * factor for k in range(2)]
 
     def finish(e, directions=range(4)):
         for d in directions:
@@ -248,7 +257,7 @@
     near1 = jnp.abs(zc_of(iota((nz, nz), 0)) - zc_of(iota((nz, nz), 1))) == 1
     beside1 = jnp.where(near1 & (iota((nz, nz), 0) < 2 * q), 1.0, 0.0).astype(bf16)
 
-    for i in (0, 3, 4):
+    for i in (0, 3):
         loads[i].wait()
 
     lane = iota((1, nz), 1)
@@ -258,10 +267,13 @@
         ids0 = jnp.where(zb == k, depth[k], ids0)
     ids1 = jnp.where(first_half((1, nz), q), ids0, roll(ids0, q, 1))
 
-    layers, size, _ = inv.shape
-    hi, lo = split(jnp.concatenate([inv[layer] for layer in range(layers)], axis=1))
-    w[:size, :] = hi
-    w[size:, :] = lo
+    for layer in range(0, layers, 2):
+        loads[4 + layer].wait()
+        loads[5 + layer].wait()
+        hi, lo = split(jnp.concatenate([inv[layer], inv[layer + 1]], axis=1))
+        at = slice(layer * size, (layer + 2) * size)
+        w[:size, at] = hi
+        w[size:, at] = lo
 
     def mix(a, b):
         side = jnp.where(b >= nz, 1, 0)
@@ -273,17 +285,16 @@
 
     smooth(src[...], x0, w, ids0, nz // 2, damping, block_in, block_out, mix_in=mix_in)
     pl.semaphore_wait(barrier, sum(jnp.where(h, 1, 0) for h in has))
-    flat = x0[...].reshape(comps * sx, sy, nz)
-    for k in range(2):
-        face = x0[:, k * (sx - 1)]
+    for k in range(2):
+        face = x0[:nf, :].reshape(fine)[:, k * (sx - 1)]
         face = pair_rows(face.reshape(comps * sy, nz), t).reshape(comps, sy // 2, nz)
         csend_x[0, k] = pack((face + roll(face, nz // 2, 2)) * 0.125)
     launch(0, (0, 1))
     for k in range(2):
-        send_y[k] = flat[:, k * (sy - 1) : k * (sy - 1) + 1]
-        face = send_y[k].reshape(comps * sx // 2, 2, 1, nz)
-        face = face[:, 0] + face[:, 1]
-        csend_y[0, k] = pack((face + roll(face, nz // 2, 2)) * 0.125)
+        face = x0[pl.ds(k * (sy - 1), comps * sx, stride=sy), :]
+        send_y[k] = face
+        face = pair_rows(face, t)
+        csend_y[0, k] = (face + roll(face, nz // 2, 1)) * 0.125
     launch(0, (2, 3))
 
     loads[1].wait()
@@ -297,40 +308,40 @@
     sig1[...] = restrict(sigma[None], t)[0]
 
     b0[...] = permute(src[...].reshape(-1, nz), to_lanes).reshape(src.shape)
-    r0[...] = residual(b0[...], x0[...], sig0[...], beside0, 1.0)
+    first = residual(b0[...], x0[:nf, :].reshape(fine), sig0[...], beside0, 1.0)
     for k in range(2):
         for h in range(2):
-            send_x[h, k] = x0[h * (comps // 2) : (h + 1) * (comps // 2), k * (sx - 1)]
-    b1[...] = restrict(r0[...], t)
+            send_x[h, k] = x0[:nf, :].reshape(fine)[h * (comps // 2) : (h + 1) * (comps // 2), k * (sx - 1)]
+    b1[:nc, :] = restrict(first, t).reshape(nc, nz)
     finish(0)
     launch(3)
-    b1[...] = add_faces(b1[...], *faces(0), 1.0)
-
-    smooth(b1[...], x1, w, ids1, q, damping * 4.0, block_in, block_out)
-    start(1, x1[...])
-    r1[...] = residual(b1[...], x1[...], sig1[...], beside1, 0.25)
+    add_faces(b1, coarse, *faces(0, 1.0))
+
+    smooth(b1[:nc, :].reshape(coarse), x1, w, ids1, q, damping * 4.0, block_in, block_out)
+    start(1, x1)
+    r1[:nc, :] = residual(b1[:nc, :].reshape(coarse), x1[:nc, :].reshape(coarse), sig1[...], beside1, 0.25).reshape(nc, nz)
     finish(1)
     launch(4, (0, 1))
-    smooth(add_faces(r1[...], *faces(1), 0.25), d1, w, ids1, q, damping * 4.0, block_in, block_out)
-    xc = x1[...] + d1[...]
-    start(2, xc)
-    cx, cy = sx // 2, sy // 2
-    spread = repeat_rows(xc.reshape(-1, nz), t).reshape(comps, cx, 1, sy, nz)
-    spread = jnp.concatenate([spread, spread], axis=2).reshape(src.shape)
-    x0[...] = x0[...] + spread
-    r0[...] = residual(b0[...], x0[...], sig0[...], beside0, 1.0)
-    out[...] = permute(x0[...].reshape(-1, nz), from_lanes).reshape(out.shape)
+    add_faces(r1, coarse, *faces(1, 0.25))
+    smooth(r1[:nc, :].reshape(coarse), d1, w, ids1, q, damping * 4.0, block_in, block_out)
+    x1[:nc, :] = x1[:nc, :] + d1[:nc, :]
+    start(2, x1)
+    cx = sx // 2
+    spread = repeat_rows(x1[:nc, :], t).reshape(comps, cx, 1, sy, nz)
+    spread = jnp.concatenate([spread, spread], axis=2).reshape(nf, nz)
+    x0[:nf, :] = x0[:nf, :] + spread
+    r0[:nf, :] = residual(b0[...], x0[:nf, :].reshape(fine), sig0[...], beside0, 1.0).reshape(nf, nz)
+    out[...] = permute(x0[:nf, :], from_lanes).reshape(fine)
     finish(3)
     finish(4, (0, 1))
     finish(2)
-    faces_x, faces_y = faces(2)
-    for k in range(2):
-        faces_x[k] = jnp.concatenate([recv_x[0, k], recv_x[1, k]], axis=0) + repeat_rows(faces_x[k].reshape(-1, nz), t).reshape(comps, sy, nz)
-        face = faces_y[k].reshape(comps * cx, 1, 1, nz)
-        faces_y[k] = recv_y[k] + jnp.concatenate([face, face], axis=1).reshape(comps * sx, 1, nz)
-    smooth(
-        add_faces(r0[...], faces_x, faces_y, 1.0), out, w, ids0, nz // 2, damping, block_in, block_out, mix_out=mix_out
-    )
+    faces_x, faces_y = faces(2, 1.0)
+    for k in range(2):
+        face = repeat_rows(faces_x[k].reshape(-1, nz), t).reshape(comps, sy, nz)
+        faces_x[k] = jnp.concatenate([recv_x[0, k], recv_x[1, k]], axis=0) + face
+        faces_y[k] = recv_y[k] + repeat_rows(faces_y[k], t)
+    add_faces(r0, fine, faces_x, faces_y)
+    smooth(r0[:nf, :].reshape(fine), out, w, ids0, nz // 2, damping, block_in, block_out, mix_out=mix_out)
     for e in range(5):
         for d in range(4 if e < 4 else 2):
             @pl.when(has[d])
@@ -349,14 +360,14 @@
         cx, cy = sx // 2, sy // 2
         vmem = pl.BlockSpec(memory_space=pltpu.VMEM)
         hbm = pl.BlockSpec(memory_space=pltpu.HBM)
-        fine, coarse = (comps, sx, sy, nz), (comps, cx, cy, nz)
+        fine = source.shape
         scratch = [
-            ((sx // 4 * (sy // 8), size, nz), f32), ((sx // 4 * (sy // 8), size, nz), f32),
-            ((2 * size, layers * size), bf16), (fine, f32), (fine, f32), (fine, f32), ((sx, sy, nz), f32), ((cx, cy, nz), f32),
-            (coarse, f32), (coarse, f32), (coarse, f32), (coarse, f32), ((comps * cx * sy, nz), f32),
+            *[((sx // 4 * (sy // 8), size + 8, nz), f32)] * 2,
+            ((2 * size, layers * size), bf16), (fine, f32), *[(((comps * sx + 1) * sy, nz), f32)] * 2, ((sx, sy, nz), f32), ((cx, cy, nz), f32),
+            *[(((comps * cx + 1) * cy, nz), f32)] * 4, ((comps * cx * sy + 8, nz), f32),
         ]
-        scratch += [((2, 2, comps // 2, sy, nz), f32)] * 2 + [((2, comps * sx, 1, nz), f32)] * 2
-        scratch += [((3, 2, comps // 2, cy, nz), f32)] * 2 + [((3, 2, comps * cx // 2, 1, nz), f32)] * 2
+        scratch += [((2, 2, comps // 2, sy, nz), f32)] * 2 + [((2, comps * sx, nz), f32)] * 2
+        scratch += [((3, 2, comps // 2, cy, nz), f32)] * 2 + [((3, 2, comps * cx, nz), f32)] * 2
         return pl.pallas_call(
             functools.partial(kernel, axes, sizes),
             out_shape=jax.ShapeDtypeStruct(source.shape, f32),
@@ -364,7 +375,7 @@
             out_specs=vmem,
             scratch_shapes=[pltpu.VMEM(source.shape, f32), pltpu.VMEM(cell_class.shape, jnp.int32)]
             + [pltpu.SMEM(class_conductivity.shape, f32), pltpu.SMEM(layer_of_depth.shape, jnp.int32)]
-            + [pltpu.VMEM(inverses.shape, f32), pltpu.SemaphoreType.DMA((5,))]
+            + [pltpu.VMEM(inverses.shape, f32), pltpu.SemaphoreType.DMA((4 + layers,))]
             + [pltpu.VMEM(s, t) for s, t in scratch]
             + [pltpu.SemaphoreType.DMA((5, 4)), pltpu.SemaphoreType.DMA((5, 4))],
             compiler_params=pltpu.CompilerParams(

time: 19.2 us -> 19.4 us (1.010)
  Pallas kernels: 18.3 us -> 18.5 us
where the time goes in v5:
time: 19.4 us; the launch traced here: 19.3 us
  Pallas kernels  18.5 us (95%)
  local copies, waits for them, and re-layouts  0.75 us (4%)
    pallas_call x1, Pallas kernels, per_device(): pl.pallas_call(functools.partial(kernel, axes, sizes), out_shape=jax.Shap...  18.5 us
    unnamed x1, local copies, waits for them, and re-layouts  0.75 us

profile of v5, /device:TPU:0, one launch (start us, length us, event | category | flops | bytes accessed | tf_op | source)
XLA Modules:
  0.0 19.3 jit_solution(11308357872785314211)
XLA Ops:
  0.0 18.5 %shard_map.55 = f32[6,8,16,128]{3,2,1,0:T(8,128)S(1)} custom-call(f32[6,8,16,128]{3,2,1,0:T(8,128)} %src_hbm.1, s32[8,16,128]{2,1,0:T(8,128)} %cls_hbm.1, f32[8]{0:T(128)} %cond_hbm.1, s32[64]{0:T(128)} %depth_hbm.1, f32[8,192,192]{2,1,0:T(8,128)} %inv_hbm.1), custom_call_target="tpu_custom_call" | custom-call | tf_op jit(solution)/shard_map/pallas_call | solution.py:371
  18.5 0.7 %copy.7 = f32[6,8,16,128]{3,2,1,0:T(8,128)} copy(f32[6,8,16,128]{3,2,1,0:T(8,128)S(1)} %shard_map.55) | data formatting | bytes 786432

commit v6 on v5

--- a/solution.py
+++ b/solution.py
@@ -94,48 +94,51 @@
     size = 2 * rows
     layers = w.shape[1] // size
     pairs = [(xb, p) for xb in range(sx // 4) for p in range(sy // 8)]
-    for at, (xb, p) in enumerate(pairs):
-        v = field[:, 4 * xb : 4 * xb + 4, 8 * p : 8 * p + 8, :].reshape(comps * 2, 2, 8, nz)
-        u0, u1 = swap_tiles(v[:, 0], v[:, 1])
-        u0, u1 = u0.reshape(rows, nz), u1.reshape(rows, nz)
-        if mix_in is None:
-            even, odd = swap_lanes(u0, u1, half)
+    pairs = list(enumerate(pairs))
+    for start in range(0, len(pairs), 2):
+        group = pairs[start : start + 2]
+        for at, (xb, p) in group:
+            v = field[:, 4 * xb : 4 * xb + 4, 8 * p : 8 * p + 8, :].reshape(comps * 2, 2, 8, nz)
+            u0, u1 = swap_tiles(v[:, 0], v[:, 1])
+            u0, u1 = u0.reshape(rows, nz), u1.reshape(rows, nz)
+            if mix_in is None:
+                even, odd = swap_lanes(u0, u1, half)
+            else:
+                mixed = permute(jnp.concatenate([u0, u1], axis=1), mix_in)
+                even, odd = mixed[:, :nz], mixed[:, nz:]
+            block_in[at, pl.ds(0, rows, stride=2), :] = even
+            block_in[at, pl.ds(1, rows, stride=2), :] = odd
+        x = jnp.concatenate([block_in[at, :size, :] for at, _ in group], axis=1)
+        hi, lo = split(x)
+        lane_ids = jnp.concatenate([ids] * len(group), axis=1)
+        twice = half < nz // 2
+        if twice:
+            x = jnp.where(first_half(x.shape, nz // 2), hi.astype(f32), x - hi.astype(f32)).astype(bf16)
+            total = dot(w[...], masked(x, lane_ids, layers))
+            total = total[:size] + total[size:]
         else:
-            mixed = permute(jnp.concatenate([u0, u1], axis=1), mix_in)
-            even, odd = mixed[:, :nz], mixed[:, nz:]
-        block_in[at, pl.ds(0, rows, stride=2), :] = even
-        block_in[at, pl.ds(1, rows, stride=2), :] = odd
-    x = jnp.concatenate([block_in[at, :size, :] for at in range(len(pairs))], axis=1)
-    hi, lo = split(x)
-    ids = jnp.concatenate([ids] * len(pairs), axis=1)
-    twice = half < nz // 2
-    if twice:
-        x = jnp.where(first_half(x.shape, nz // 2), hi.astype(f32), x - hi.astype(f32)).astype(bf16)
-        total = dot(w[...], masked(x, ids, layers))
-        total = total[:size] + total[size:]
-    else:
-        total = dot(w[...], masked(hi, ids, layers))
-        total = total[:size] + total[size:] + dot(w[:size, :], masked(lo, ids, layers))
-    total = total * scale
-    for at, (xb, p) in enumerate(pairs):
-        block = total[:, at * nz : (at + 1) * nz]
-        block_out[at, :size, :] = block + roll(block, nz // 2, 1) if twice else block
-        even = block_out[at, pl.ds(0, rows, stride=2), :]
-        odd = block_out[at, pl.ds(1, rows, stride=2), :]
-        if mix_out is None:
-            u0, u1 = swap_lanes(even, odd, half)
-        else:
-            mixed = permute(jnp.concatenate([even, odd], axis=1), mix_out)
-            u0, u1 = mixed[:, :nz], mixed[:, nz:]
-        v0, v1 = swap_tiles(u0.reshape(comps * 2, 8, nz), u1.reshape(comps * 2, 8, nz))
-        v = jnp.stack([v0, v1], axis=1).reshape(comps, 4, 8, nz)
-        if mix_out is None:
-            for c in range(comps):
-                for i in range(4):
-                    out_ref[pl.ds((c * sx + 4 * xb + i) * sy + 8 * p, 8), :] = v[c, i]
-        else:
-            at = (slice(None), slice(4 * xb, 4 * xb + 4), slice(8 * p, 8 * p + 8), slice(None))
-            out_ref[at] = out_ref[at] + v
+            total = dot(w[...], masked(hi, lane_ids, layers))
+            total = total[:size] + total[size:] + dot(w[:size, :], masked(lo, lane_ids, layers))
+        total = total * scale
+        for at, (xb, p) in group:
+            block = total[:, (at - start) * nz : (at - start + 1) * nz]
+            block_out[at, :size, :] = block + roll(block, nz // 2, 1) if twice else block
+            even = block_out[at, pl.ds(0, rows, stride=2), :]
+            odd = block_out[at, pl.ds(1, rows, stride=2), :]
+            if mix_out is None:
+                u0, u1 = swap_lanes(even, odd, half)
+            else:
+                mixed = permute(jnp.concatenate([even, odd], axis=1), mix_out)
+                u0, u1 = mixed[:, :nz], mixed[:, nz:]
+            v0, v1 = swap_tiles(u0.reshape(comps * 2, 8, nz), u1.reshape(comps * 2, 8, nz))
+            v = jnp.stack([v0, v1], axis=1).reshape(comps, 4, 8, nz)
+            if mix_out is None:
+                for c in range(comps):
+                    for i in range(4):
+                        out_ref[pl.ds((c * sx + 4 * xb + i) * sy + 8 * p, 8), :] = v[c, i]
+            else:
+                at = (slice(None), slice(4 * xb, 4 * xb + 4), slice(8 * p, 8 * p + 8), slice(None))
+                out_ref[at] = out_ref[at] + v
 
 
 def residual(b, u, sigma, beside_z, factor):
@@ -178,7 +181,7 @@
     comps, sx, sy, nz = src.shape
     named = ((src_hbm, src), (cls_hbm, cls), (cond_hbm, cond), (depth_hbm, depth))
     layers, size, _ = inv.shape
-    named += tuple((inv_hbm.at[layer], inv.at[layer]) for layer in range(layers))
+    named += ((inv_hbm, inv),)
     loads = [pltpu.make_async_copy(a, b, in_sem.at[i]) for i, (a, b) in enumerate(named)]
     for load in loads:
         load.start()
@@ -257,7 +260,7 @@
     near1 = jnp.abs(zc_of(iota((nz, nz), 0)) - zc_of(iota((nz, nz), 1))) == 1
     beside1 = jnp.where(near1 & (iota((nz, nz), 0) < 2 * q), 1.0, 0.0).astype(bf16)
 
-    for i in (0, 3):
+    for i in (0, 3, 4):
         loads[i].wait()
 
     lane = iota((1, nz), 1)
@@ -267,13 +270,9 @@
         ids0 = jnp.where(zb == k, depth[k], ids0)
     ids1 = jnp.where(first_half((1, nz), q), ids0, roll(ids0, q, 1))
 
-    for layer in range(0, layers, 2):
-        loads[4 + layer].wait()
-        loads[5 + layer].wait()
-        hi, lo = split(jnp.concatenate([inv[layer], inv[layer + 1]], axis=1))
-        at = slice(layer * size, (layer + 2) * size)
-        w[:size, at] = hi
-        w[size:, at] = lo
+    hi, lo = split(jnp.concatenate([inv[layer] for layer in range(layers)], axis=1))
+    w[:size, :] = hi
+    w[size:, :] = lo
 
     def mix(a, b):
         side = jnp.where(b >= nz, 1, 0)
@@ -375,7 +374,7 @@
             out_specs=vmem,
             scratch_shapes=[pltpu.VMEM(source.shape, f32), pltpu.VMEM(cell_class.shape, jnp.int32)]
             + [pltpu.SMEM(class_conductivity.shape, f32), pltpu.SMEM(layer_of_depth.shape, jnp.int32)]
-            + [pltpu.VMEM(inverses.shape, f32), pltpu.SemaphoreType.DMA((4 + layers,))]
+            + [pltpu.VMEM(inverses.shape, f32), pltpu.SemaphoreType.DMA((5,))]
             + [pltpu.VMEM(s, t) for s, t in scratch]
             + [pltpu.SemaphoreType.DMA((5, 4)), pltpu.SemaphoreType.DMA((5, 4))],
             compiler_params=pltpu.CompilerParams(

time: 19.4 us -> 20.5 us (1.057)
  Pallas kernels: 18.5 us -> 19.6 us
    pallas_call x1, Pallas kernels: 18.5 us -> 19.6 us  [per_device(): pl.pallas_call(functools.partial(kernel, axes, sizes), out_shape=jax.Shap...]
where the time goes in v6:
time: 20.5 us; the launch traced here: 20.4 us
  Pallas kernels  19.6 us (96%)
  local copies, waits for them, and re-layouts  0.75 us (4%)
    pallas_call x1, Pallas kernels, per_device(): pl.pallas_call(functools.partial(kernel, axes, sizes), out_shape=jax.Shap...  19.6 us
    unnamed x1, local copies, waits for them, and re-layouts  0.75 us

profile of v6, /device:TPU:0, one launch (start us, length us, event | category | flops | bytes accessed | tf_op | source)
XLA Modules:
  0.0 20.4 jit_solution(12857250003661687086)
XLA Ops:
  0.0 19.6 %shard_map.55 = f32[6,8,16,128]{3,2,1,0:T(8,128)S(1)} custom-call(f32[6,8,16,128]{3,2,1,0:T(8,128)} %src_hbm.1, s32[8,16,128]{2,1,0:T(8,128)} %cls_hbm.1, f32[8]{0:T(128)} %cond_hbm.1, s32[64]{0:T(128)} %depth_hbm.1, f32[8,192,192]{2,1,0:T(8,128)} %inv_hbm.1), custom_call_target="tpu_custom_call" | custom-call | tf_op jit(solution)/shard_map/pallas_call | solution.py:370
  19.6 0.7 %copy.7 = f32[6,8,16,128]{3,2,1,0:T(8,128)} copy(f32[6,8,16,128]{3,2,1,0:T(8,128)S(1)} %shard_map.55) | data formatting | bytes 786432

commit v7 on v4

--- a/solution.py
+++ b/solution.py
@@ -88,7 +88,7 @@
     return jnp.concatenate(out, axis=0)
 
 
-def smooth(field, out_ref, w, ids, half, scale, block_in, block_out, mix_in=None, mix_out=None):
+def smooth(field, out_ref, w, w_row, ids, half, scale, block_in, block_out, mix_in=None, mix_out=None):
     comps, sx, sy, nz = field.shape
     rows = comps * 16
     size = 2 * rows
@@ -114,8 +114,8 @@
         total = total[:size] + total[size:]
         total = total[:, :n] + total[:, n:]
     else:
-        total = dot(w[...], masked(hi, ids, layers))
-        total = total[:size] + total[size:] + dot(w[:size, :], masked(lo, ids, layers))
+        high = masked(hi, ids, layers)
+        total = dot(w_row[...], jnp.concatenate([high, high, masked(lo, ids, layers)], axis=0))
     total = total * scale
     for at, (xb, p) in enumerate(pairs):
         block_out[at] = total[:, at * nz : (at + 1) * nz]
@@ -167,7 +167,7 @@
 
 def kernel(
     axes, sizes, src_hbm, cls_hbm, cond_hbm, depth_hbm, inv_hbm, out,
-    src, cls, cond, depth, inv, in_sem, block_in, block_out, w, b0, x0, r0, sig0, sig1, b1, x1, r1, d1, t,
+    src, cls, cond, depth, inv, in_sem, block_in, block_out, w, w_row, b0, x0, r0, sig0, sig1, b1, x1, r1, d1, t,
     send_x, recv_x, send_y, recv_y, csend_x, crecv_x, csend_y, crecv_y, send_sem, recv_sem,
 ):
     comps, sx, sy, nz = src.shape
@@ -262,6 +262,8 @@
     hi, lo = split(jnp.concatenate([inv[layer] for layer in range(layers)], axis=1))
     w[:size, :] = hi
     w[size:, :] = lo
+    for k, part in enumerate((hi, lo, hi)):
+        w_row[:, k * layers * size : (k + 1) * layers * size] = part
 
     def mix(a, b):
         side = jnp.where(b >= nz, 1, 0)
@@ -271,7 +273,7 @@
     wide = (2 * nz, 2 * nz)
     mix_in, mix_out = mix(iota(wide, 0), iota(wide, 1)), mix(iota(wide, 1), iota(wide, 0))
 
-    smooth(src[...], x0, w, ids0, nz // 2, damping, block_in, block_out, mix_in=mix_in)
+    smooth(src[...], x0, w, w_row, ids0, nz // 2, damping, block_in, block_out, mix_in=mix_in)
     pl.semaphore_wait(barrier, sum(jnp.where(h, 1, 0) for h in has))
     flat = x0[...].reshape(comps * sx, sy, nz)
     for k in range(2):
@@ -306,12 +308,12 @@
     launch(3)
     b1[...] = add_faces(b1[...], *faces(0), 1.0)
 
-    smooth(b1[...], x1, w, ids1, q, damping * 4.0, block_in, block_out)
+    smooth(b1[...], x1, w, w_row, ids1, q, damping * 4.0, block_in, block_out)
     start(1, x1[...])
     r1[...] = residual(b1[...], x1[...], sig1[...], beside1, 0.25)
     finish(1)
     launch(4, (0, 1))
-    smooth(add_faces(r1[...], *faces(1), 0.25), d1, w, ids1, q, damping * 4.0, block_in, block_out)
+    smooth(add_faces(r1[...], *faces(1), 0.25), d1, w, w_row, ids1, q, damping * 4.0, block_in, block_out)
     xc = x1[...] + d1[...]
     start(2, xc)
     cx, cy = sx // 2, sy // 2
@@ -329,7 +331,7 @@
         face = faces_y[k].reshape(comps * cx, 1, 1, nz)
         faces_y[k] = recv_y[k] + jnp.concatenate([face, face], axis=1).reshape(comps * sx, 1, nz)
     smooth(
-        add_faces(r0[...], faces_x, faces_y, 1.0), out, w, ids0, nz // 2, damping, block_in, block_out, mix_out=mix_out
+        add_faces(r0[...], faces_x, faces_y, 1.0), out, w, w_row, ids0, nz // 2, damping, block_in, block_out, mix_out=mix_out
     )
     for e in range(5):
         for d in range(4 if e < 4 else 2):
@@ -352,7 +354,7 @@
         fine, coarse = (comps, sx, sy, nz), (comps, cx, cy, nz)
         scratch = [
             ((sx // 4 * (sy // 8), size, nz), f32), ((sx // 4 * (sy // 8), size, nz), f32),
-            ((2 * size, layers * size), bf16), (fine, f32), (fine, f32), (fine, f32), ((sx, sy, nz), f32), ((cx, cy, nz), f32),
+            ((2 * size, layers * size), bf16), ((size, 3 * layers * size), bf16), (fine, f32), (fine, f32), (fine, f32), ((sx, sy, nz), f32), ((cx, cy, nz), f32),
             (coarse, f32), (coarse, f32), (coarse, f32), (coarse, f32), ((comps * cx * sy, nz), f32),
         ]
         scratch += [((2, 2, comps // 2, sy, nz), f32)] * 2 + [((2, comps * sx, 1, nz), f32)] * 2

time: 19.2 us -> 19.3 us (level)
  no operation moved by 1% of the time
where the time goes in v7:
time: 19.3 us; the launch traced here: 19.2 us
  Pallas kernels  18.4 us (95%)
  local copies, waits for them, and re-layouts  0.75 us (4%)
    pallas_call x1, Pallas kernels, per_device(): pl.pallas_call(functools.partial(kernel, axes, sizes), out_shape=jax.Shap...  18.4 us
    unnamed x1, local copies, waits for them, and re-layouts  0.75 us

profile of v7, /device:TPU:0, one launch (start us, length us, event | category | flops | bytes accessed | tf_op | source)
XLA Modules:
  0.0 19.2 jit_solution(139307107210527860)
XLA Ops:
  0.0 18.4 %shard_map.55 = f32[6,8,16,128]{3,2,1,0:T(8,128)S(1)} custom-call(f32[6,8,16,128]{3,2,1,0:T(8,128)} %src_hbm.1, s32[8,16,128]{2,1,0:T(8,128)} %cls_hbm.1, f32[8]{0:T(128)} %cond_hbm.1, s32[64]{0:T(128)} %depth_hbm.1, f32[8,192,192]{2,1,0:T(8,128)} %inv_hbm.1), custom_call_target="tpu_custom_call" | custom-call | tf_op jit(solution)/shard_map/pallas_call | solution.py:362
  18.4 0.7 %copy.7 = f32[6,8,16,128]{3,2,1,0:T(8,128)} copy(f32[6,8,16,128]{3,2,1,0:T(8,128)S(1)} %shard_map.55) | data formatting | bytes 786432
